TPU v7x, 32 devices: a whole 2x2x4 slice. The times are simulated.
32 devices in a mesh: tm: 4 (over x, core), slot: 8 (over z, y).
Axes of the slice: x: 2, y: 2, z: 4, core: 2. Of those that a mesh axis runs over, the one named last changes fastest.
Arguments:
- inputs: bfloat16 [8, 1536, 512], P('slot', 'tm'), may hold values from -6 to 6
- cotangent: bfloat16 [8, 1536, 512], P('slot', 'tm'), may hold values from -6 to 6
- lengths: int32 [8], P('slot'), may hold values from 48 to 1512, as said below
- weight_noise: bfloat16 [32, 196608], P(('tm', 'slot')), may hold values from -0.25 to 0.25
- ffn1_in: bfloat16 [512, 2048], replicated, may hold values from -0.25 to 0.25
- ffn1_out: bfloat16 [2048, 512], replicated, may hold values from -0.125 to 0.125
- query_w: bfloat16 [512, 512], replicated, may hold values from -0.25 to 0.25
- key_w: bfloat16 [512, 512], replicated, may hold values from -0.25 to 0.25
- value_w: bfloat16 [512, 512], replicated, may hold values from -0.25 to 0.25
- pos_w: bfloat16 [512, 512], replicated, may hold values from -0.25 to 0.25
- out_w: bfloat16 [512, 512], replicated, may hold values from -2 to 2
- conv_in: bfloat16 [512, 1024], replicated, may hold values from -0.25 to 0.25
- conv_out: bfloat16 [512, 512], replicated, may hold values from -0.25 to 0.25
- ffn2_in: bfloat16 [512, 2048], replicated, may hold values from -0.25 to 0.25
- ffn2_out: bfloat16 [2048, 512], replicated, may hold values from -0.125 to 0.125
- conv_kernel: float32 [32, 512], replicated, may hold values from -1 to 1
- ffn1_gain: float32 [512], replicated, may hold values from 0.5 to 1.5
- attn_gain: float32 [512], replicated, may hold values from 0.5 to 1.5
- conv_gain: float32 [512], replicated, may hold values from 0.5 to 1.5
- ffn2_gain: float32 [512], replicated, may hold values from 0.5 to 1.5
- final_gain: float32 [512], replicated, may hold values from 0.5 to 1.5
- bn_gain: float32 [512], replicated, may hold values from 0.5 to 1.5
- bn_bias: float32 [512], replicated, may hold values from -3 to 3
- pos_u: float32 [512], replicated, may hold values from -3 to 3
- pos_v: float32 [512], replicated, may hold values from -3 to 3
Outputs:
- output: bfloat16 [8, 1536, 512], P('slot', 'tm')
- input_grad: bfloat16 [8, 1536, 512], P('slot', 'tm')
- ffn1_in_grad: float32 [512, 2048], replicated
- ffn1_out_grad: float32 [2048, 512], replicated
- query_grad: float32 [512, 512], replicated
- key_grad: float32 [512, 512], replicated
- value_grad: float32 [512, 512], replicated
- pos_grad: float32 [512, 512], replicated
- out_grad: float32 [512, 512], replicated
- conv_in_grad: float32 [512, 1024], replicated
- conv_out_grad: float32 [512, 512], replicated
- ffn2_in_grad: float32 [512, 2048], replicated
- ffn2_out_grad: float32 [2048, 512], replicated
- kernel_grad: float32 [32, 512], replicated
- ffn1_gain_grad: float32 [512], replicated
- attn_gain_grad: float32 [512], replicated
- conv_gain_grad: float32 [512], replicated
- ffn2_gain_grad: float32 [512], replicated
- final_gain_grad: float32 [512], replicated
- bn_gain_grad: float32 [512], replicated
- bn_bias_grad: float32 [512], replicated
- pos_u_grad: float32 [512], replicated
- pos_v_grad: float32 [512], replicated
Inputs may be any that keep to these rules, and one draw needn't show every extreme that they name: `lengths`: among the 1 slots of each index of slot, one, drawn from the seed, has the largest length 1512.
All inputs are finite; a program needn't handle non-finite values.
Results may differ from a plain program's by a relative error of at most 0.029.
Values may be sent and summed in bfloat16 or wider, within the bound.
A program may use at most 256 MiB of HBM per device.

v0:
```python
import math

import jax
import jax.numpy as jnp
from jax import lax
from jax.experimental import pallas as pl
from jax.experimental.pallas import tpu as pltpu
from jax.sharding import PartitionSpec as P

H = 8
HD = 64
LANE = 128
F32 = jnp.float32
BF = jnp.bfloat16
EPS = 1e-05
FILL = -1e30
VMEM_LIMIT = 60 * 2**20


def dot(a, b):
    return lax.dot_general(a, b, (((1,), (0,)), ((), ())), preferred_element_type=F32)


def dot_nt(a, b):
    return lax.dot_general(a, b, (((1,), (1,)), ((), ())), preferred_element_type=F32)


def dot_tn(a, b):
    return lax.dot_general(a, b, (((0,), (0,)), ((), ())), preferred_element_type=F32)


def norm_parts(v):
    mean = jnp.mean(v, axis=-1, keepdims=True)
    cen = v - mean
    r = lax.rsqrt(jnp.mean(cen * cen, axis=-1, keepdims=True) + EPS)
    return cen * r, r


def norm(v, gain):
    u, _ = norm_parts(v)
    return u * gain


def norm_back(v, gain, e):
    u, r = norm_parts(v)
    eg = e * gain
    back = r * (eg - jnp.mean(eg, axis=-1, keepdims=True) - u * jnp.mean(eg * u, axis=-1, keepdims=True))
    return back, jnp.sum(e * u, axis=0, keepdims=True)


def sigmoid(v):
    return 1.0 / (1.0 + jnp.exp(-v))


def swish_and_slope(v):
    s = sigmoid(v)
    sv = s * v
    return sv, s + sv * (1.0 - s)


def cols(p, width=LANE):
    return pl.ds(pl.multiple_of(p * width, width), width)


def lane_half(e):
    lane = lax.broadcasted_iota(jnp.int32, (1, LANE), 1)
    return (lane < HD) if e == 0 else (lane >= HD)


def call(body, outs, ins, scratch=(), name=None):
    return pl.pallas_call(
        body,
        out_shape=[jax.ShapeDtypeStruct(s, d) for s, d in outs],
        in_specs=[
            pl.BlockSpec(memory_space=pltpu.SMEM) if x.dtype == jnp.int32 else pl.BlockSpec(memory_space=pltpu.VMEM)
            for x in ins
        ],
        out_specs=[pl.BlockSpec(memory_space=pltpu.VMEM) for _ in outs],
        scratch_shapes=list(scratch),
        compiler_params=pltpu.CompilerParams(vmem_limit_bytes=VMEM_LIMIT),
        name=name,
    )(*ins)


MESH = pl.DeviceIdType.MESH


class Place:
    def __init__(self):
        tms, slots = lax.axis_size("tm"), lax.axis_size("slot")
        wide = 1 << ((slots.bit_length() - 1) // 2)
        self.size = {"c": 2, "x": tms // 2, "y": wide, "z": slots // wide}
        self.tm, self.slot = lax.axis_index("tm"), lax.axis_index("slot")
        self.at = {
            "c": lax.rem(self.tm, 2),
            "x": lax.div(self.tm, 2),
            "y": lax.rem(self.slot, wide),
            "z": lax.div(self.slot, wide),
        }

    def peer(self, axis, off):
        pos = dict(self.at)
        pos[axis] = lax.rem(pos[axis] + off, self.size[axis])
        return (pos["x"] * 2 + pos["c"], pos["z"] * self.size["y"] + pos["y"]), pos[axis]

    def peers(self, axis):
        return [(off,) + self.peer(axis, off) for off in range(1, self.size[axis])]

    def greet(self, axes):
        bar = pltpu.get_barrier_semaphore()
        count = 0
        for axis in axes:
            for _, dev, _ in self.peers(axis):
                pl.semaphore_signal(bar, inc=1, device_id=dev, device_id_type=MESH)
                count += 1
        pl.semaphore_wait(bar, count)


def rows_at(start, size):
    return pl.ds(pl.multiple_of(start, 16), size)


def add_into(dst, start, lanes, terms, size):
    step = 64 if size % 64 == 0 else 16

    def one(i, carry):
        off = pl.multiple_of(i * step, step)
        total = terms[0](off, step).astype(F32)
        for term in terms[1:]:
            total = total + term(off, step).astype(F32)
        dst[pl.ds(pl.multiple_of(start + off, 16), step), lanes] = total.astype(dst.dtype)
        return carry

    lax.fori_loop(0, size // step, one, 0)


GROUP = 2048


class Flow:
    STAGES = 9

    @staticmethod
    def lane_parts(order, size):
        rows = GROUP // 2
        for axis in order[:2]:
            rows //= size[axis]
        return max(1, 16 * size[order[2]] // rows)

    @staticmethod
    def scratch(order, width, size, kind):
        shapes, sends = [], 2
        blk = GROUP // 2
        parts = Flow.lane_parts(order, size)
        for lv, axis in enumerate(order):
            n = size[axis]
            blk = blk * parts // n if lv == 2 else blk // n
            w = width // parts if lv == 2 else width
            if (kind != "front" or lv == 0) and (kind != "back" or lv > 0):
                shapes.append(pltpu.VMEM((n - 1, blk, w), BF))
            sends += 2 * (n - 1)
        if kind != "front":
            shapes.append(pltpu.VMEM((blk, width // parts), BF))
        sems = pltpu.SemaphoreType.DMA((sends,))
        return shapes + [sems, sems, pltpu.SemaphoreType.DMA((1,))]

    def __init__(self, pc, order, lane, width, kind, src, own, core, out, first, bufs):
        self.ssem, self.rsem, self.lsem = bufs[-3:]
        bufs = list(bufs[:-3])
        self.used, self.now = 0, 2 if kind == "back" else 0
        self.made, self.local = [], []
        size = pc.size
        lanes = pl.ds(lane, width)
        c = pc.at["c"]
        top = GROUP // 2
        parts = self.lane_parts(order, size)
        blk, rel = [top], [0]
        for lv, axis in enumerate(order):
            if lv < 2:
                blk.append(blk[-1] // size[axis])
                rel.append(rel[-1] + pc.at[axis] * blk[-1])
        low = blk[2] * parts // size[order[2]]

        def share(pos):
            if parts == 1:
                return rel[2] + pos * low, lanes
            at = pl.multiple_of(lane + lax.rem(pos, parts) * (width // parts), LANE)
            return rel[2] + lax.div(pos, parts) * low, pl.ds(at, width // parts)

        ((_, cdev, _),) = pc.peers("c")
        into = [None] * 3
        if kind != "back":
            into[0] = bufs.pop(0)
        if kind != "front":
            into[1], into[2], fin = bufs
        core_copy = [self.copy(lambda: src.at[rows_at((1 - c) * top, top), lanes], lambda: core.at[:, lanes], cdev)]
        down = []
        for lv, axis in enumerate(order):
            cps = []
            for off, dev, pos in pc.peers(axis):
                if lv < 2:
                    s = lambda lv=lv, pos=pos: core.at[rows_at(rel[lv] + pos * blk[lv + 1], blk[lv + 1]), lanes]
                else:
                    s = lambda pos=pos: core.at[rows_at(share(pos)[0], low), share(pos)[1]]
                cps.append(self.copy(s, lambda lv=lv, off=off: into[lv].at[off - 1], dev))
            down.append(cps)
        mine = share(pc.at[order[2]])
        out_share = lambda: out.at[rows_at(first + c * top + mine[0], low), mine[1]]
        out_at = lambda lv: out.at[rows_at(first + c * top + rel[lv], blk[lv]), lanes]
        up = [[self.copy(lambda: fin, out_share, dev) for _, dev, _ in pc.peers(order[2])]]
        for lv in (2, 1):
            up.append([self.copy(lambda lv=lv: out_at(lv), lambda lv=lv: out_at(lv), dev) for _, dev, _ in pc.peers(order[lv - 1])])
        up.append([self.copy(lambda: out_at(0), lambda: out_at(0), cdev)])

        def fold(lv):
            if lv == 0:
                add_into(core, 0, lanes, [lambda o, n: own(o, n, lanes), lambda o, n: core[pl.ds(o, n), lanes]], top)
                return
            row, ln, size_ = (mine + (low,)) if lv == 3 else (rel[lv], lanes, blk[lv])
            terms = [lambda o, n: core[pl.ds(pl.multiple_of(row + o, 16), n), ln]]
            for k in range(size[order[lv - 1]] - 1):
                terms.append(lambda o, n, k=k: into[lv - 1][k, pl.ds(o, n), :])
            if lv == 3:
                add_into(fin, 0, slice(None), terms, size_)
            else:
                add_into(core, row, lanes, terms, size_)

        keep = lambda: pltpu.make_async_copy(fin, out_share(), self.lsem.at[0])

        def s1():
            self.arrived(core_copy)
            fold(0)
            self.start(down[0])

        def s2():
            if kind != "back":
                self.arrived(down[0])
                fold(1)
            if kind != "front":
                self.start(down[1])

        def s3():
            self.arrived(down[1])
            fold(2)
            self.start(down[2])

        def s4():
            self.arrived(down[2])
            fold(3)
            keep().start()
            self.start(up[0])

        def climb(i):
            def run():
                if i == 0:
                    keep().wait()
                self.arrived(up[i])
                if i < 3:
                    self.start(up[i + 1])

            return run

        self.stages = [lambda: self.start(core_copy), s1, s2, s3, s4] + [climb(i) for i in range(4)]
        self.last = 3 if kind == "front" else self.STAGES
        self.sent = {"front": core_copy + down[0], "back": down[1] + down[2] + sum(up, []), "whole": core_copy + sum(down + up, [])}[kind]

    def copy(self, src, dst, dev):
        k = self.used
        self.used += 1
        return src, dst, k, dev

    def make(self, cp):
        src, dst, k, dev = cp
        return pltpu.make_async_remote_copy(
            src_ref=src(), dst_ref=dst(), send_sem=self.ssem.at[k], recv_sem=self.rsem.at[k], device_id=dev, device_id_type=MESH
        )

    def start(self, cps):
        for cp in cps:
            self.make(cp).start()

    def arrived(self, cps):
        for cp in cps:
            self.make(cp).wait_recv()

    def finish(self):
        for cp in self.sent:
            self.make(cp).wait_send()

    def take(self):
        if self.now >= self.last:
            return lambda: None
        self.now += 1
        return self.stages[self.now - 1]


def advance(flows):
    for flow in flows:
        flow.take()()


EARLY = ((("y", "x", "z"), 0, 384), (("x", "y", "z"), 384, 128))
EVEN = ((("y", "x", "z"), 0, 256), (("x", "y", "z"), 256, 256))


ZFIRST = ((("z", "x", "y"), 0, 256), (("z", "y", "x"), 256, 256))
LASTA = ((("y", "x", "z"), 0, 256), (("x", "y", "z"), 256, 128), (("z", "x", "y"), 384, 128))
LASTB = ((("y", "x", "z"), 0, 128), (("x", "y", "z"), 128, 256), (("z", "y", "x"), 384, 128))
MID = {"f2i": 2048, "f2o": 4096, "o": 0}
FRONT = ("f2i",)
LAYOUT = {"f2i": EVEN, "f2o": EVEN, "o": EVEN, "q": LASTA, "f1i": LASTB, "f1o": EVEN}
TICKS = {0: "f2o o", 4: "f2i", 9: "f2o o", 10: "f2i", 16: "f2o o", 17: "f2i", 19: "f2o o f2i q"}
REST = ("f2i", "f2o", "o", "q", "f1o", "f1i")


def lanes_of(size, wanted):
    return wanted if max(Flow.lane_parts(order, size) for order, _, _ in wanted) == 1 else EVEN


def flow_scratch(size, layout, kind):
    return [Flow.scratch(order, width, size, kind) for order, _, width in lanes_of(size, layout)]


def flat_list(lists):
    return [x for part in lists for x in part]


class Taker:
    def __init__(self, refs):
        self.refs = list(refs)

    def __call__(self, n):
        got, self.refs = self.refs[:n], self.refs[n:]
        return got


def make_flows(pc, layout, kind, src, own, core, out, first, taker):
    flows = []
    for (order, lane, width), shapes in zip(lanes_of(pc.size, layout), flow_scratch(pc.size, layout, kind)):
        flows.append(Flow(pc, order, lane, width, kind, src, own, core, out, first, taker(len(shapes))))
    return flows


FLAT = {"f1i": 0, "f1o": 2048, "q": 4096, "k": 4608, "v": 5120, "p": 5632, "o": 6144, "ci": 6656, "co": 7680, "f2i": 8192, "f2o": 10240}
FLAT_ROWS = 12288
ORDER = tuple(FLAT)
FOLDS = {"f1i": 4, "ci": 2, "f2i": 4}
FLAT_SIZE = {n: (list(FLAT.values()) + [FLAT_ROWS])[i + 1] - FLAT[n] for i, n in enumerate(FLAT)}


def ticks(point, plan, p):
    for at, run in plan.items():
        if at % 2 == point:
            pl.when(p == at // 2)(lambda run=run: (run(), None)[1])


class Gather:
    @staticmethod
    def scratch(size, shard_rows, width):
        part, pieces = Gather.cut(shard_rows)
        links = 2 * pieces * sum(n - 1 for n in size.values())
        sems = pltpu.SemaphoreType.DMA((links,))
        return [
            pltpu.VMEM((size["x"], 2, size["z"], size["y"], shard_rows, width), BF),
            pltpu.VMEM((width // LANE, 64, LANE), F32),
            sems,
            sems,
        ]

    @staticmethod
    def cut(shard_rows):
        part = 64 if shard_rows % 64 == 0 else 16
        return part, shard_rows // part

    def __init__(self, pc, wf, bufs):
        self.pc, self.wf = pc, wf
        self.nb, self.scr, self.ssem, self.rsem = bufs
        self.shard_rows = self.nb.shape[4]
        self.part, self.pieces = self.cut(self.shard_rows)
        self.xs = pc.size["x"]
        self.used = 0
        self.stages = [self.plan(hx, q) for hx in range(2) for q in range(self.pieces)]

    def copies(self, ref, axis):
        out = []
        for off, dev, _ in self.pc.peers(axis):
            k = self.used
            self.used += 1
            out.append(
                (off, pltpu.make_async_remote_copy(
                    src_ref=ref, dst_ref=ref, send_sem=self.ssem.at[k], recv_sem=self.rsem.at[k], device_id=dev, device_id_type=MESH
                ))
            )
        return out

    def plan(self, hx, q):
        pc, nb = self.pc, self.nb
        x, c, z, y = (pc.at[a] for a in "xczy")
        rows = pl.ds(q * self.part, self.part)
        side = pl.ds(hx * (self.xs // 2), self.xs // 2)
        in_half = lambda pos: lax.div(pos, self.xs // 2) == hx
        along = {
            "x": self.copies(nb.at[x, c, z, y, rows], "x"),
            "z": self.copies(nb.at[side, c, z, y, rows], "z"),
            "y": self.copies(nb.at[side, c, :, y, rows], "y"),
            "c": self.copies(nb.at[side, c, :, :, rows], "c"),
        }

        def each(axis, what, cond=None):
            for off, cp in along[axis]:
                if cond is None:
                    getattr(cp, what)()
                else:
                    pl.when(cond(off))(lambda cp=cp: getattr(cp, what)())

        sends = lambda off: in_half(x)
        gets = lambda off: in_half(lax.rem(x - off + self.xs, self.xs))

        def end():
            each("c", "wait_recv")
            if self.part == 64:
                self.mix_half(hx, q)
            elif q == self.pieces - 1:
                self.mix_half(hx, None)

        def done():
            each("x", "wait_send", sends)
            for axis in "zyc":
                each(axis, "wait_send")

        return {
            "X": lambda: each("x", "start", sends),
            "Z": lambda: (each("x", "wait_recv", gets), each("z", "start")),
            "Y": lambda: (each("z", "wait_recv"), each("y", "start")),
            "C": lambda: (each("y", "wait_recv"), each("c", "start")),
            "E": end,
            "D": done,
        }

    def run(self, ops):
        for op in ops:
            if 0 <= op[1] < len(self.stages):
                self.stages[op[1]][op[0]]()

    def finish(self):
        for stages in self.stages:
            stages["D"]()

    def noise_at(self, row):
        pc = self.pc
        got = []
        sub = min(64, self.part)
        for i in range(64 // sub):
            at = row + i * sub
            d = lax.div(at, self.shard_rows)
            slots = pc.size["z"] * pc.size["y"]
            tm, sl = lax.div(d, slots), lax.rem(d, slots)
            off = pl.multiple_of(lax.rem(at, self.shard_rows), 16)
            got.append(
                self.nb[lax.div(tm, 2), lax.rem(tm, 2), lax.div(sl, pc.size["y"]), lax.rem(sl, pc.size["y"]), pl.ds(off, sub), :].astype(F32)
            )
        return got[0] if len(got) == 1 else jnp.concatenate(got, axis=0)

    def mix(self, row, base, size, fold):
        wf, scr = self.wf, self.scr
        value = self.noise_at(row)
        if fold == 1:
            at = rows_at(row, 64)
            wf[at, :] = (wf[at, :].astype(F32) + value).astype(BF)
            return
        for b in range(512 // LANE):
            scr[b] = value[:, b * LANE : (b + 1) * LANE]
        high = 64 // fold
        for j in range(fold):
            at = rows_at(base + j * (size // fold) + lax.div(row - base, fold), high)
            for b in range(512 // LANE):
                lanes = pl.ds(b * LANE, LANE)
                wf[at, lanes] = (wf[at, lanes].astype(F32) + scr[b, pl.ds(j, high, stride=fold), :]).astype(BF)

    def mix_half(self, hx, q):
        for name in ORDER:
            base, size, fold = FLAT[name], FLAT_SIZE[name], FOLDS.get(name, 1)
            if (base < FLAT_ROWS // 2) != (hx == 0):
                continue
            begin, end = base // 64, (base + size) // 64
            start, stride = (begin, 1) if q is None else (begin + (q - begin) % self.pieces, self.pieces)
            lax.fori_loop(
                0, (end - start + stride - 1) // stride,
                lambda i, t: (self.mix((start + i * stride) * 64, base, size, fold), t)[1], 0,
            )


class KeysAll:
    @staticmethod
    def scratch(xs):
        n = 2 * xs - 1
        sems = pltpu.SemaphoreType.DMA((H // 2, n))
        return [sems, sems]

    def __init__(self, pc, kv, bufs):
        self.pc, self.kv = pc, kv
        self.ssem, self.rsem = bufs

    def copy(self, p, k, tm, dev):
        ref = self.kv.at[p, :, tm]
        return pltpu.make_async_remote_copy(
            src_ref=ref, dst_ref=ref, send_sem=self.ssem.at[p, k], recv_sem=self.rsem.at[p, k], device_id=dev, device_id_type=MESH
        )

    def core(self, p):
        ((_, dev, _),) = self.pc.peers("c")
        return [self.copy(p, 0, self.pc.tm, dev)]

    def line(self, p):
        return [self.copy(p, off, self.pc.tm, dev) for off, dev, _ in self.pc.peers("x")]

    def relay(self, p):
        ((_, dev, _),) = self.pc.peers("c")
        xs = self.pc.size["x"]
        out = []
        for off in range(1, xs):
            source = lax.rem(self.pc.at["x"] - off + xs, xs) * 2 + self.pc.at["c"]
            out.append(self.copy(p, xs - 1 + off, source, dev))
        return out

    def send(self, p):
        for cp in self.core(p):
            cp.start()

    def send_line(self, p):
        for cp in self.line(p):
            cp.start()

    def forward(self, p):
        for come, on in zip(self.line(p), self.relay(p)):
            come.wait_recv()
            on.start()

    def ready(self, p):
        for cp in self.core(p) + self.relay(p):
            cp.wait_recv()

    def sent(self, p):
        for cp in self.line(p) + self.core(p) + self.relay(p):
            cp.wait_send()


def angle_tables(hi, lo, rates):
    for ref, step in ((hi, 64.0), (lo, 1.0)):
        count = ref.shape[1]
        angle = lax.broadcasted_iota(jnp.int32, (count, rates.shape[1]), 0).astype(F32) * step * rates
        ref[0] = jnp.sin(angle)
        ref[1] = jnp.cos(angle)


def angle_block(hi, lo, m):
    hs, hc = hi[0, pl.ds(m, 1), :], hi[1, pl.ds(m, 1), :]
    ls, lc = lo[0], lo[1]
    return hs * lc + hc * ls, hc * lc - hs * ls


def early_body(*refs):
    lens, noise, raws = refs[0], refs[1], refs[2:13]
    x_ref, gain1, gain2, pos_u, pos_v = refs[13:18]
    wn, x1_out, pre_out, a2_out, qu_out, qv_out, kv_out, trig_out, sin_out, cos_out, att_out, probs = refs[18:30]
    wf, flat, x1_ref, pre_ref, a2_ref, qu, qv, kv, trig, sin, cos, hi, lo, att, pbuf, wsem, osem, psem = refs[30:48]
    bufs = refs[48:]
    pc = Place()
    rows, width = x_ref.shape
    half = width // 2
    tms = lax.axis_size("tm")
    frames = rows * tms
    loads = []
    for name, raw in zip(ORDER, raws):
        for j in range(FOLDS.get(name, 1)):
            size = FLAT_SIZE[name] // FOLDS.get(name, 1)
            dst = wf.at[pl.ds(FLAT[name] + j * size, size), :]
            loads.append(pltpu.make_async_copy(raw.at[:, pl.ds(j * 512, 512)], dst, wsem.at[len(loads)]))
            loads[-1].start()
    gather = Gather(pc, wf, bufs[:4])
    keys = KeysAll(pc, kv, bufs[4:6])

    def unfold(i, carry):
        for r in range(8):
            for b in range(width // LANE):
                at = pl.ds(pl.multiple_of((i * 8 + r) * width + b * LANE, LANE), LANE)
                flat[b, pl.ds(i * 8 + r, 1), :] = noise[:, at].astype(F32)
        return carry

    shard_rows = gather.shard_rows
    lax.fori_loop(0, shard_rows // 8, unfold, 0)
    for b in range(width // LANE):
        gather.nb[pc.at["x"], pc.at["c"], pc.at["z"], pc.at["y"], :, pl.ds(b * LANE, LANE)] = flat[b].astype(BF)
    pc.greet("cxyz")
    n = gather.pieces
    gather.run([("X", i) for i in range(2 * n)])
    gather.run([("Z", 0), ("Z", 1)])
    rates = jnp.exp(lax.broadcasted_iota(jnp.int32, (1, half), 1).astype(F32) * (-2.0 * math.log(10000.0) / width))
    angle_tables(hi, lo, rates)

    def angles(m, carry):
        s, c = angle_block(hi, lo, m)
        at = rows_at(m * 64, 64)
        trig[at, pl.ds(0, half)] = s.astype(BF)
        trig[at, pl.ds(half, half)] = c.astype(BF)
        return carry

    def own_angles(m, carry):
        s, c = angle_block(hi, lo, pc.tm * (rows // 64) + m)
        sin[rows_at(m * 64, 64), :] = s
        cos[rows_at(m * 64, 64), :] = c
        return carry

    lax.fori_loop(0, frames // 64, angles, 0)
    lax.fori_loop(0, rows // 64, own_angles, 0)
    for cp in loads:
        cp.wait()
    outs = []

    def put(src, dst):
        cp = pltpu.make_async_copy(src, dst, osem.at[len(outs)])
        cp.start()
        outs.append(cp)

    x = x_ref[...].astype(F32)
    a1 = norm(x, gain1[...]).astype(BF)
    for t in range(2, n + 1):
        gather.run([("Z", t), ("Y", t - 2), ("C", t - 3), ("E", t - 4)])
    gather.run([("Y", n - 1), ("C", n - 2), ("E", n - 3), ("C", n - 1), ("E", n - 2), ("Z", n + 1), ("E", n - 1)])
    part = lambda name: wf.at[pl.ds(FLAT[name], FLAT_SIZE[name]), :]
    x1 = x + 0.5 * ffn_forward(a1, part("f1i"), part("f1o"), pre_ref)
    x1_ref[...] = x1
    a2 = norm(x1, gain2[...]).astype(BF)
    a2_ref[...] = a2
    k = dot(a2, part("k")[...]).astype(BF)
    v = dot(a2, part("v")[...]).astype(BF)
    for p in range(H // 2):
        kv[p, 0, pc.tm] = k[:, p * LANE : (p + 1) * LANE]
        kv[p, 1, pc.tm] = v[:, p * LANE : (p + 1) * LANE]
        if p == 0:
            keys.send_line(0)
        keys.send(p)
    gather.run([("Z", n + 2), ("Y", n)])
    q = dot(a2, part("q")[...])
    scale = HD**-0.5
    qu[...] = ((q + pos_u[...]).astype(BF).astype(F32) * scale).astype(BF)
    qv[...] = ((q + pos_v[...]).astype(BF).astype(F32) * scale).astype(BF)
    for src, dst in ((x1_ref, x1_out), (pre_ref, pre_out), (a2_ref, a2_out), (qu, qu_out), (qv, qv_out), (trig, trig_out), (sin, sin_out), (cos, cos_out)):
        put(src, dst)
    put(wf.at[pl.ds(0, FLAT_ROWS // 2), :], wn.at[pl.ds(0, FLAT_ROWS // 2), :])
    steps = {
        0: "Y1 Z3", 1: "Y2 Z4 C0", 2: "C1 E0", 3: "Y3 Z5 E1", 4: "Y4 C2", 5: "C3 E2", 6: "Y5 E3", 7: "C4", 8: "C5 E4 E5",
    }
    if n != 6:
        steps = {8: " ".join("%s%d" % (op, i) for op, low in (("Z", 3), ("Y", 1), ("C", 0), ("E", 0)) for i in range(low, n))}
    steps = {at: [(op[0], n + int(op[1:])) for op in text.split()] for at, text in steps.items()}
    plan = {at: (lambda ops=ops: gather.run(ops)) for at, ops in steps.items() if at < H}
    ok = lax.broadcasted_iota(jnp.int32, (1, frames), 1) < lens[0]
    w_pos = part("p")
    store = lambda p, e: pltpu.make_async_copy(pbuf.at[e], probs.at[2 * p + e], psem.at[e])

    def pair(p, carry):
        at = cols(p)
        mixed = None
        for e in range(2):
            mine = lane_half(e)
            qve = jnp.where(mine, qv[:, at], jnp.zeros((), BF))
            que = jnp.where(mine, qu[:, at], jnp.zeros((), BF))
            a_s = dot_nt(qve, w_pos[pl.ds(0, half), at])
            a_c = dot_nt(qve, w_pos[pl.ds(half, half), at])
            b_c = (a_s * sin[...] + a_c * cos[...]).astype(BF)
            b_s = (a_c * sin[...] - a_s * cos[...]).astype(BF)
            if e == 0:
                pl.when(p == 1)(lambda: keys.send_line(3))
            else:
                pl.when(p == 0)(lambda: keys.send_line(2))
            s = dot_nt(b_s, trig[:, pl.ds(0, half)]) + dot_nt(b_c, trig[:, pl.ds(half, half)])
            if e == 0:
                pl.when(p == 0)(lambda: (keys.forward(0), keys.send_line(1))[1])
                keys.ready(p)
            s = s + dot_nt(que, kv[p, 0].reshape(frames, LANE))
            s = jnp.where(ok, s, FILL)
            m = jnp.max(s, axis=-1, keepdims=True)
            ex = jnp.exp(s - m)
            tot = jnp.sum(ex, axis=-1, keepdims=True)
            low = (ex * (1.0 / tot)).astype(BF)
            pl.when(p > 0)(lambda: store(p - 1, e).wait())
            pbuf[e] = low
            store(p, e).start()
            got = dot(low, kv[p, 1].reshape(frames, LANE))
            mixed = got if e == 0 else jnp.where(mine, got, mixed)
            if e == 1:
                pl.when(p < H // 2 - 1)(lambda: keys.forward(p + 1))
            ticks(e, plan, p)
        att[:, at] = mixed.astype(BF)
        return carry

    lax.fori_loop(0, H // 2, pair, 0)
    put(kv, kv_out)
    put(att, att_out)
    gather.run(steps[8])
    put(wf.at[pl.ds(FLAT_ROWS // 2, FLAT_ROWS // 2), :], wn.at[pl.ds(FLAT_ROWS // 2, FLAT_ROWS // 2), :])
    for e in range(2):
        store(H // 2 - 1, e).wait()
    for p in range(H // 2):
        keys.sent(p)
    gather.finish()
    for cp in outs:
        cp.wait()


def chunk(c):
    return pl.ds(pl.multiple_of(c * 512, 512), 512)


def ffn_forward(normed, w_in, w_out, pre_ref):
    def one(c, acc):
        pre = dot(normed, w_in[chunk(c), :])
        pre_ref[:, chunk(c)] = pre
        return acc + dot((pre * sigmoid(pre)).astype(BF), w_out[chunk(c), :])

    return lax.fori_loop(0, w_in.shape[0] // 512, one, jnp.zeros((normed.shape[0], w_out.shape[1]), F32))


def ffn_through(g_low, w_in, w_out, pre_ref, hid_ref, dpre_ref):
    def one(c, acc):
        sw, slope = swish_and_slope(pre_ref[:, chunk(c)])
        hid_ref[:, chunk(c)] = sw.astype(BF)
        dpre = (dot_nt(g_low, w_out[chunk(c), :]) * slope).astype(BF)
        dpre_ref[:, chunk(c)] = dpre
        return acc + dot_nt(dpre, w_in[chunk(c), :])

    return lax.fori_loop(0, w_in.shape[0] // 512, one, jnp.zeros(g_low.shape, F32))


def ffn_in_grad(normed, dpre_ref, gin_ref):
    normed_t = normed.T

    def one(c, carry):
        gin_ref[chunk(c), :] = dot(normed_t, dpre_ref[:, chunk(c)]).astype(gin_ref.dtype)
        return carry

    lax.fori_loop(0, gin_ref.shape[0] // 512, one, 0)


def ffn_out_grad(g_low, hid_ref, gout_ref):
    def one(c, carry):
        gout_ref[chunk(c), :] = dot_tn(hid_ref[:, chunk(c)], g_low).astype(gout_ref.dtype)
        return carry

    lax.fori_loop(0, gout_ref.shape[0] // 512, one, 0)


def ffn_hidden(pre_ref, hid_ref):
    def one(c, carry):
        pre = pre_ref[:, chunk(c)]
        hid_ref[:, chunk(c)] = (pre * sigmoid(pre)).astype(BF)
        return carry

    lax.fori_loop(0, pre_ref.shape[1] // 512, one, 0)


class Fetch:
    def __init__(self, sems):
        self.sems, self.n = sems, 0

    def __call__(self, src, dst):
        cp = pltpu.make_async_copy(src, dst, self.sems.at[self.n])
        self.n += 1
        cp.start()
        return cp


def part_of(wn, name):
    return wn.at[pl.ds(FLAT[name], FLAT_SIZE[name]), :]


def valid_rows(lens, rows):
    first = lax.axis_index("tm") * rows
    return ((first + lax.broadcasted_iota(jnp.int32, (rows, 1), 0)) < lens[0]).astype(F32)


def spread(ext, start, value):
    value = value.astype(F32)
    for b in range(ext.shape[0]):
        ext[b, pl.ds(start, value.shape[0]), :] = value[:, b * LANE : (b + 1) * LANE]


def tap_sum(ext, taps, out_ref, offset):
    count = taps.shape[0]
    rows = out_ref.shape[0]
    block = 64 if rows % 64 == 0 else 16

    def one(i, carry):
        for b in range(ext.shape[0]):
            at = pl.ds(b * LANE, LANE)
            acc = jnp.zeros((block, LANE), F32)
            for k in range(count):
                acc = acc + taps[pl.ds(k, 1), at] * ext[b, pl.ds(i * block + offset(k), block), :]
            out_ref[pl.ds(pl.multiple_of(i * block, block), block), at] = acc
        return carry

    lax.fori_loop(0, rows // block, one, 0)


def bn_stats(sums):
    total = sums[2:3, :]
    mu = sums[0:1, :] / total
    var = sums[1:2, :] / total - mu * mu
    return mu, lax.rsqrt(var + EPS), total


class Totals:
    @staticmethod
    def scratch(tms, slots, width):
        n = tms + slots - 2
        return [
            pltpu.VMEM((tms, 8, width), F32),
            pltpu.VMEM((slots, 8, width), F32),
            pltpu.SemaphoreType.DMA((n,)),
            pltpu.SemaphoreType.DMA((n,)),
        ]

    def __init__(self, pc, bufs):
        self.pc, self.bufs = pc, bufs

    def begin(self, value):
        self.sent = []
        self.cps = self.send(0, value)

    def turn(self):
        self.cps = self.send(1, self.end(0))

    def done(self):
        value = self.end(1)
        for cp in self.sent:
            cp.wait_send()
        return value

    def send(self, i, value):
        pc, buf = self.pc, self.bufs[i]
        ssem, rsem = self.bufs[2:]
        me = (pc.tm, pc.slot)[i]
        buf[me] = value
        n = buf.shape[0]
        for off in range(1, n):
            to = lax.rem(me + off, n)
            k = off - 1 + i * (self.bufs[0].shape[0] - 1)
            cp = pltpu.make_async_remote_copy(
                src_ref=buf.at[me], dst_ref=buf.at[me], send_sem=ssem.at[k], recv_sem=rsem.at[k],
                device_id=(to, pc.slot) if i == 0 else (pc.tm, to), device_id_type=MESH,
            )
            cp.start()
            self.sent.append(cp)
        return self.sent[-(n - 1) :]

    def end(self, i):
        for cp in self.cps:
            cp.wait_recv()
        buf = self.bufs[i]
        value = buf[0]
        for j in range(1, buf.shape[0]):
            value = value + buf[j]
        return value


def greet_rows(pc, tms, slots):
    bar = pltpu.get_barrier_semaphore()
    for off in range(1, tms):
        pl.semaphore_signal(bar, inc=1, device_id=(lax.rem(pc.tm + off, tms), pc.slot), device_id_type=MESH)
    for off in range(1, slots):
        pl.semaphore_signal(bar, inc=1, device_id=(pc.tm, lax.rem(pc.slot + off, slots)), device_id_type=MESH)
    pl.semaphore_wait(bar, tms + slots - 2)


def middle_body(
    lens, att, x1_ref, cot, wn, taps, bn_gain, bn_bias, gain3, gain4, gain5,
    out_h, dx2_h, datt_h, g_h, smalls_ref, bns_ref, cores,
    w_o, w_ci, w_co, w_f2i, w_f2o, fsem, early, late, hsem, gm_ref, ddwo_ref, z_ref, ext, ext2, dwo_ref, pre_ref, dgm_ref, acc, x2_ref, core, out_ref, dx2_ref, datt_ref, g_ref, hid_ref, dpre_ref, csem, *bufs,
):
    pc = Place()
    tms, slots = lax.axis_size("tm"), lax.axis_size("slot")
    rows, width = x1_ref.shape
    count = taps.shape[0]
    fetch, put = Fetch(fsem), Fetch(csem)
    outs = []
    got = {n: fetch(part_of(wn, n), d) for n, d in (("o", w_o), ("ci", w_ci), ("co", w_co), ("f2i", w_f2i), ("f2o", w_f2o))}
    greet_rows(pc, tms, slots)
    taker = Taker(bufs)
    totals = Totals(pc, taker(4)), Totals(pc, taker(4))
    flows = []
    for i, name in enumerate(FRONT):
        src = g_ref.at[pl.ds(MID[name], GROUP), :]
        half_rows = lambda o, n, lanes, src=src: src[pl.ds(pl.multiple_of(pc.at["c"] * (GROUP // 2) + o, 16), n), lanes]
        flows += make_flows(pc, LAYOUT[name], "front", src, half_rows, core.at[i], None, 0, taker)

    def halo(src, dst, k, step):
        dev = (lax.rem(pc.tm + step + tms, tms), pc.slot)
        return pltpu.make_async_remote_copy(
            src_ref=src, dst_ref=dst, send_sem=hsem.at[2 * k], recv_sem=hsem.at[2 * k + 1], device_id=dev, device_id_type=MESH
        )

    got["o"].wait()
    x2 = x1_ref[...] + dot(att[...], w_o[...])
    x2_ref[...] = x2
    a3 = norm(x2, gain3[...]).astype(BF)
    got["ci"].wait()
    z1 = dot(a3, w_ci[pl.ds(0, width), :])
    z2 = dot(a3, w_ci[pl.ds(width, width), :])
    z_ref[:, pl.ds(0, width)] = z1
    z_ref[:, pl.ds(width, width)] = z2
    ok = valid_rows(lens, rows)
    gm_ref[...] = (z1 * sigmoid(z2) * ok).astype(BF)
    cp = halo(gm_ref.at[pl.ds(rows - count, count), :], early, 0, 1)
    cp.start()
    spread(ext, count, gm_ref[...])
    cp.wait()
    spread(ext, 0, jnp.where(pc.tm > 0, early[...], jnp.zeros((), BF)))
    tap_sum(ext, taps, dwo_ref, lambda k: k + 1)
    dwo = dwo_ref[...]
    dwv = dwo * ok
    totals[0].begin(
        jnp.concatenate(
            [
                jnp.sum(dwv, axis=0, keepdims=True),
                jnp.sum(dwv * dwv, axis=0, keepdims=True),
                jnp.zeros((1, width), F32) + jnp.sum(ok, axis=0, keepdims=True),
                jnp.zeros((5, width), F32),
            ],
            axis=0,
        )
    )
    totals[0].turn()
    sums = totals[0].done()
    mu, inv, total = bn_stats(sums)
    xhat = (dwo_ref[...] - mu) * inv
    sw, slope = swish_and_slope(xhat * bn_gain[...] + bn_bias[...])
    sw = sw.astype(BF)
    got["co"].wait()
    x3 = x2_ref[...] + dot(sw, w_co[...])
    a4 = norm(x3, gain4[...]).astype(BF)
    got["f2i"].wait()
    got["f2o"].wait()
    x4 = x3 + 0.5 * ffn_forward(a4, w_f2i, w_f2o, pre_ref)
    out_ref[...] = norm(x4, gain5[...]).astype(BF)
    outs.append(put(out_ref, out_h))
    dx4, gg5 = norm_back(x4, gain5[...], cot[...].astype(F32))
    g4 = (0.5 * dx4).astype(BF)
    lo = FLAT["o"]
    da4 = ffn_through(g4, w_f2i, w_f2o, pre_ref, hid_ref, dpre_ref)
    back, gg4 = norm_back(x3, gain4[...], da4)
    dx3 = dx4 + back
    g3 = dx3.astype(BF)
    dbn = dot_nt(g3, w_co[...]) * slope
    totals[1].begin(
        jnp.concatenate(
            [jnp.sum(dbn * xhat, axis=0, keepdims=True), jnp.sum(dbn, axis=0, keepdims=True), jnp.zeros((6, width), F32)], axis=0
        )
    )
    part = lambda name: g_ref.at[pl.ds(MID[name], GROUP), :]
    ffn_in_grad(a4, dpre_ref, part("f2i"))
    totals[1].turn()
    advance(flows)
    ffn_out_grad(g4, hid_ref, part("f2o"))
    g_ref[pl.ds(FLAT["co"] - lo, width), :] = dot_tn(sw, g3).astype(BF)
    for name in ("f2i", "f2o"):
        if name not in FRONT:
            outs.append(put(part(name), g_h.at[pl.ds(MID[name], GROUP), :]))
    sums2 = totals[1].done()
    bns_ref[...] = sums2
    ddwo_ref[...] = (bn_gain[...] * inv * (dbn - ok * (sums2[1:2, :] + xhat * sums2[0:1, :]) / total)).astype(BF)
    cp = halo(ddwo_ref.at[pl.ds(0, count), :], late, 1, -1)
    cp.start()
    advance(flows)
    spread(ext2, 0, ddwo_ref[...])
    cp.wait()
    spread(ext2, rows, jnp.where(pc.tm < tms - 1, late[...], jnp.zeros((), BF)))
    tap_sum(ext2, taps, dgm_ref, lambda k: count - 1 - k)
    block = 64 if rows % 64 == 0 else 16
    for b in range(ext.shape[0]):
        acc[...] = jnp.zeros(acc.shape, F32)

        def one(i, carry, b=b):
            mine = ext2[b, pl.ds(pl.multiple_of(i * block, block), block), :]
            for k in range(count):
                prod = mine * ext[b, pl.ds(i * block + k + 1, block), :]
                acc[k] = acc[k] + jnp.sum(prod.reshape(block // 8, 8, LANE), axis=0)
            return carry

        lax.fori_loop(0, rows // block, one, 0)
        smalls_ref[pl.ds(0, count), pl.ds(b * LANE, LANE)] = jnp.sum(acc[...], axis=1)
    z1 = z_ref[:, pl.ds(0, width)]
    sg = sigmoid(z_ref[:, pl.ds(width, width)])
    dg = dgm_ref[...] * ok
    dz1 = (dg * sg).astype(BF)
    dz2 = (dg * z1 * sg * (1.0 - sg)).astype(BF)
    a3t = norm(x2_ref[...], gain3[...]).astype(BF).T
    g_ref[pl.ds(FLAT["ci"] - lo, width), :] = dot(a3t, dz1).astype(BF)
    g_ref[pl.ds(FLAT["ci"] - lo + width, width), :] = dot(a3t, dz2).astype(BF)
    da3 = dot_nt(dz1, w_ci[pl.ds(0, width), :]) + dot_nt(dz2, w_ci[pl.ds(width, width), :])
    back, gg3 = norm_back(x2_ref[...], gain3[...], da3)
    dx2 = dx3 + back
    dx2_ref[...] = dx2
    outs.append(put(dx2_ref, dx2_h))
    g2 = dx2.astype(BF)
    g_ref[pl.ds(0, width), :] = dot_tn(att[...], g2).astype(BF)
    outs.append(put(g_ref.at[pl.ds(0, GROUP), :], g_h.at[pl.ds(0, GROUP), :]))
    datt_ref[...] = dot_nt(g2, w_o[...]).astype(BF)
    outs.append(put(datt_ref, datt_h))
    advance(flows)
    outs.append(put(core, cores))
    smalls_ref[pl.ds(count, 8), :] = jnp.concatenate([gg3, gg4, gg5, jnp.zeros((5, width), F32)], axis=0)
    for flow in flows:
        flow.finish()
    for cp in outs:
        cp.wait()


class Butterfly:
    @staticmethod
    def scratch(devices, shape):
        n = devices.bit_length() - 1
        return [pltpu.VMEM((n,) + shape, F32), pltpu.SemaphoreType.DMA((n,)), pltpu.SemaphoreType.DMA((n,))]

    def __init__(self, pc, value, bufs):
        self.value, (self.got, self.ssem, self.rsem) = value, bufs
        self.devs = []
        for axis, me in (("tm", pc.tm), ("slot", pc.slot)):
            bit = 1
            while bit < lax.axis_size(axis):
                to = me + bit - 2 * bit * lax.rem(lax.div(me, bit), 2)
                self.devs.append((to, pc.slot) if axis == "tm" else (pc.tm, to))
                bit *= 2

    def copy(self, k):
        return pltpu.make_async_remote_copy(
            src_ref=self.value, dst_ref=self.got.at[k], send_sem=self.ssem.at[k], recv_sem=self.rsem.at[k],
            device_id=self.devs[k], device_id_type=MESH,
        )

    def stage(self, k):
        if k > 0:
            self.copy(k - 1).wait()
            self.value[...] = self.value[...] + self.got[k - 1]
        if k < len(self.devs):
            self.copy(k).start()


GROUP = 2048


class KeyGrads:
    @staticmethod
    def scratch(tms, rows):
        pairs, xs = H // 2, tms // 2
        sems = pltpu.SemaphoreType.DMA((pairs, xs + 1))
        return [
            pltpu.VMEM((pairs, 2, 2, tms, HD, rows), BF),
            pltpu.VMEM((pairs, 2, tms, HD, rows), BF),
            pltpu.VMEM((xs - 1, pairs, 2, 2, HD, rows), BF),
            pltpu.VMEM((pairs, 2, 2, HD, rows), BF),
            pltpu.VMEM((pairs, 2, HD, rows), BF),
            sems,
            sems,
        ]

    def __init__(self, pc, bufs):
        self.pc = pc
        self.mine, self.core, self.line, self.both, self.got, self.ssem, self.rsem = bufs

    def put(self, p, kind, e, value):
        rows = self.mine.shape[-1]
        for t in range(self.mine.shape[3]):
            self.mine[p, kind, e, t] = value[:, t * rows : (t + 1) * rows].astype(BF)

    def copy(self, p, k, src, dst, dev):
        return pltpu.make_async_remote_copy(
            src_ref=src, dst_ref=dst, send_sem=self.ssem.at[p, k], recv_sem=self.rsem.at[p, k], device_id=dev, device_id_type=MESH
        )

    def first(self, p):
        ((_, dev, _),) = self.pc.peers("c")
        return [self.copy(p, 0, self.mine.at[p, :, 1 - self.pc.at["c"]], self.core.at[p], dev)]

    def second(self, p):
        return [
            self.copy(p, off, self.core.at[p, :, pl.ds(2 * pos, 2)], self.line.at[off - 1, p], dev) for off, dev, pos in self.pc.peers("x")
        ]

    def third(self, p):
        ((_, dev, _),) = self.pc.peers("c")
        return [self.copy(p, self.pc.size["x"], self.both.at[p, :, 1 - self.pc.at["c"]], self.got.at[p], dev)]

    def step(self, p, i):
        c, x = self.pc.at["c"], self.pc.at["x"]
        if i == 1:
            for cp in self.first(p):
                cp.wait_recv()
            for kind in range(2):
                for t in range(self.core.shape[2]):
                    total = self.core[p, kind, t].astype(F32) + self.mine[p, kind, c, t].astype(F32)
                    self.core[p, kind, t] = total.astype(BF)
        if i == 2:
            for cp in self.second(p):
                cp.wait_recv()
            for kind in range(2):
                for t in range(2):
                    total = self.core[p, kind, 2 * x + t].astype(F32)
                    for j in range(self.line.shape[0]):
                        total = total + self.line[j, p, kind, t].astype(F32)
                    self.both[p, kind, t] = total.astype(BF)
        if i == 3:
            for cp in self.third(p):
                cp.wait_recv()
            return
        for cp in (self.first, self.second, self.third)[i](p):
            cp.start()

    def sent(self, p):
        for cp in self.first(p) + self.second(p) + self.third(p):
            cp.wait_send()

    def collect(self, p, kind, dst):
        c = self.pc.at["c"]
        own = self.both[p, kind, c]
        other = self.got[p, kind]
        dst[pl.ds(pl.multiple_of(p * LANE + c * HD, HD), HD), :] = own
        dst[pl.ds(pl.multiple_of(p * LANE + (1 - c) * HD, HD), HD), :] = other


def late_body(
    qu_h, qv_h, kv_h, wn, trig_h, sin_h, cos_h, probs, datt_h, att_h, g_mid, cores_h, a2_h, x1_h, dx2_h, x_h, pre_h, smalls2, gain2, gain1,
    dx0_ref, flat, total_ref,
    qu, qv, kv, w_p, trig, sin, cos, datt, att, a2, x1_ref, dx2_ref, x_ref, wqkv, own, core, psem, fsem,
    dq_ref, dkt, dvt, gpost, qut, qvt, datt_t, g_low, *bufs,
):
    pc = Place()
    rows = qu.shape[0]
    half = sin.shape[1]
    fetch = Fetch(fsem)
    c = pc.at["c"]
    whole = [name for name in MID if name not in FRONT]
    owns = [fetch(g_mid.at[rows_at(MID[name] + c * (GROUP // 2), GROUP // 2), :], own.at[i]) for i, name in enumerate(whole)]
    owns += [fetch(cores_h.at[i], core.at[i]) for i in range(len(FRONT))]
    early = [fetch(s, d) for s, d in ((qu_h, qu), (qv_h, qv), (datt_h, datt), (kv_h, kv), (att_h, att), (part_of(wn, "p"), w_p), (trig_h, trig), (sin_h, sin), (cos_h, cos))]
    later = [
        fetch(s, d)
        for s, d in (
            (a2_h, a2), (x1_h, x1_ref), (dx2_h, dx2_ref), (x_h, x_ref), (wn.at[pl.ds(FLAT["q"], 1536), :], wqkv),
        )
    ]
    pc.greet("cxyz")
    taker = Taker(bufs)
    keys = KeyGrads(pc, taker(7))
    fly = Butterfly(pc, total_ref, taker(3))
    groups = {}
    for i, name in enumerate(FRONT):
        groups[name] = make_flows(pc, LAYOUT[name], "back", None, None, core.at[i], flat, FLAT[name], taker)
    for i, name in enumerate(whole):
        mine = lambda o, n, lanes, i=i: own[i, pl.ds(o, n), lanes]
        src = g_mid.at[pl.ds(MID[name], GROUP), :]
        groups[name] = make_flows(pc, LAYOUT[name], "whole", src, mine, core.at[len(FRONT) + i], flat, FLAT[name], taker)
    for i, name in enumerate(("q", "f1i", "f1o")):
        at = FLAT[name]
        mine = lambda o, n, lanes, at=at: g_low[pl.ds(pl.multiple_of(at + c * (GROUP // 2) + o, 16), n), lanes]
        groups[name] = make_flows(pc, LAYOUT[name], "whole", g_low.at[pl.ds(at, GROUP), :], mine, core.at[3 + i], flat, at, taker)
    for cp in owns:
        cp.wait()
    for name in MID:
        advance(groups[name])
    for cp in early:
        cp.wait()
    qut[...] = qu[...].T
    qvt[...] = qv[...].T
    datt_t[...] = datt[...].T

    def run(members):
        stages = [flow.take() for name in members.split() for flow in groups[name]]
        return lambda: [stage() for stage in stages]

    plan = {at: run(members) for at, members in sorted(TICKS.items()) if at < 2 * H}
    after = lambda point: run(TICKS.get(point, ""))()
    scale = HD**-0.5

    def scores(p, pbuf, load):
        at = cols(p)
        for e in range(2):
            mine = lane_half(e)
            part = pl.ds(pl.multiple_of(p * LANE + e * HD, HD), HD)
            dm = jnp.where(mine, datt[:, at], jnp.zeros((), BF))
            inner = jnp.sum(dm.astype(F32) * att[:, at].astype(F32), axis=-1, keepdims=True)
            dp = dot_nt(dm, kv[p, 1].reshape(-1, LANE))
            load(2 * p + e).wait()
            low_p = pbuf[2 * p + e]
            ds = (low_p.astype(F32) * (dp - inner)).astype(BF)
            pbuf[2 * p + e] = ds
            keys.put(p, 0, e, dot(qut[part, :], ds))
            keys.put(p, 1, e, dot(datt_t[part, :], low_p))
            if e == 0:
                pl.when(p > 0)(lambda: keys.step(p - 1, 1))
            else:
                keys.step(p, 0)
            ticks(e, plan, p)

    def queries(p, pbuf):
        at = cols(p)
        dqu = dqv = None
        for e in range(2):
            mine = lane_half(e)
            part = pl.ds(pl.multiple_of(p * LANE + e * HD, HD), HD)
            ds = pbuf[2 * p + e]
            db_s = dot(ds, trig[:, pl.ds(0, half)])
            db_c = dot(ds, trig[:, pl.ds(half, half)])
            da_s = (db_c * sin[...] - db_s * cos[...]).astype(BF)
            da_c = (db_c * cos[...] + db_s * sin[...]).astype(BF)
            gpost[part, pl.ds(0, half)] = dot(qvt[part, :], da_s)
            gpost[part, pl.ds(half, half)] = dot(qvt[part, :], da_c)
            part_v = dot(da_s, w_p[pl.ds(0, half), at]) + dot(da_c, w_p[pl.ds(half, half), at])
            part_u = dot(ds, kv[p, 0].reshape(-1, LANE))
            dqu = part_u if e == 0 else jnp.where(mine, part_u, dqu)
            dqv = part_v if e == 0 else jnp.where(mine, part_v, dqv)
            if e == 0:
                pl.when(p == 0)(lambda: keys.step(last, 1))
            else:
                keys.step(p, 2)
            ticks(e, plan, p + H // 2)
        dqu = dqu * scale
        dqv = dqv * scale
        dq_ref[:, at] = (dqu + dqv).astype(BF)
        total_ref[pl.ds(37, 1), at] = jnp.sum(dqu, axis=0, keepdims=True)
        total_ref[pl.ds(38, 1), at] = jnp.sum(dqv, axis=0, keepdims=True)

    def attention(pbuf):
        load = lambda h: pltpu.make_async_copy(probs.at[h], pbuf.at[h], psem.at[h])
        for h in range(H):
            load(h).start()
        lax.fori_loop(0, H // 2, lambda p, t: (scores(p, pbuf, load), t)[1], 0)
        lax.fori_loop(0, H // 2, lambda p, t: (queries(p, pbuf), t)[1], 0)

    last = H // 2 - 1
    pl.run_scoped(attention, pltpu.VMEM((H, rows, kv.shape[2] * rows), BF))
    def tail(pre_ref, w1, hid_ref, dpre_ref):
        last_in = [fetch(pre_h, pre_ref), fetch(wn.at[pl.ds(0, 4096), :], w1)]
        g_low[pl.ds(FLAT["p"], 512), :] = gpost[...].T.astype(BF)
        for cp in later:
            cp.wait()
        a2t = a2[...].T
        g_low[pl.ds(FLAT["q"], 512), :] = dot(a2t, dq_ref[...]).astype(BF)
        da2 = dot_nt(dq_ref[...], wqkv[pl.ds(0, 512), :])
        after(16)
        for p in range(H // 2):
            keys.step(p, 3)
            keys.collect(p, 0, dkt)
            keys.collect(p, 1, dvt)
        g_low[pl.ds(FLAT["k"], 512), :] = dot_nt(a2t, dkt[...]).astype(BF)
        g_low[pl.ds(FLAT["v"], 512), :] = dot_nt(a2t, dvt[...]).astype(BF)
        advance(groups["q"])
        after(17)
        for cp in last_in:
            cp.wait()
        ffn_hidden(pre_ref, hid_ref)
        da2 = da2 + dot_nt(dkt[...].T, wqkv[pl.ds(512, 512), :]) + dot_nt(dvt[...].T, wqkv[pl.ds(1024, 512), :])
        back, gg2 = norm_back(x1_ref[...], gain2[...], da2)
        dx1 = dx2_ref[...] + back
        g1 = (0.5 * dx1).astype(BF)
        x = x_ref[...].astype(F32)
        a1 = norm(x, gain1[...]).astype(BF)
        after(18)
        ffn_out_grad(g1, hid_ref, g_low.at[pl.ds(2048, 2048), :])
        advance(groups["f1o"])
        da1 = ffn_through(g1, w1.at[pl.ds(0, 2048), :], w1.at[pl.ds(2048, 2048), :], pre_ref, hid_ref, dpre_ref)
        ffn_in_grad(a1, dpre_ref, g_low.at[pl.ds(0, 2048), :])
        advance(groups["f1i"])
        after(19)
        back, gg1 = norm_back(x, gain1[...], da1)
        dx0_ref[...] = (dx1 + back).astype(BF)
        total_ref[pl.ds(smalls2.shape[0] - 5, 2), :] = jnp.concatenate([gg1, gg2], axis=0)

    pl.run_scoped(tail, pltpu.VMEM(pre_h.shape, F32), pltpu.VMEM((4096, 512), BF), pltpu.VMEM(pre_h.shape, BF), pltpu.VMEM(pre_h.shape, BF))
    count = smalls2.shape[0] - 8
    total_ref[pl.ds(0, count), :] = smalls2[pl.ds(0, count), :]
    total_ref[pl.ds(count, 3), :] = smalls2[pl.ds(count, 3), :]
    total_ref[pl.ds(count + 7, 1), :] = jnp.zeros((1, 512), F32)
    flows = flat_list(list(groups.values()))
    t = 0
    while any(flow.now < flow.last for flow in flows) or t <= len(fly.devs):
        advance([flow for i in range(4) for name in REST if i < len(groups[name]) for flow in groups[name][i : i + 1]])
        if t <= len(fly.devs):
            fly.stage(t)
        t += 1
    for p in range(H // 2):
        keys.sent(p)
    for flow in flows:
        flow.finish()


def widen_body(flat, total, bns, *refs):
    outs, smalls, (ibuf, obuf, isem, osem) = refs[:11], refs[11:21], refs[21:]
    count = smalls[0].shape[0]
    smalls[0][...] = total[pl.ds(0, count), :]
    for i, ref in enumerate(smalls[1:8]):
        ref[...] = total[pl.ds(count + i, 1), :]
    for i, ref in enumerate(smalls[8:]):
        ref[...] = bns[pl.ds(i, 1), :]
    step = 512
    n = FLAT_ROWS // step
    loads = [pltpu.make_async_copy(flat.at[pl.ds(i * step, step), :], ibuf.at[i], isem.at[i]) for i in range(n)]
    for cp in loads:
        cp.start()
    stores = []
    slots = obuf.shape[0]
    for i in range(n):
        name = [m for m in ORDER if FLAT[m] <= i * step][-1]
        out = outs[ORDER.index(name)]
        off = i * step - FLAT[name]
        fold = FOLDS.get(name, 1)
        if fold == 1:
            dst = out.at[pl.ds(off, step), :]
        else:
            dst = out.at[:, pl.ds(off, step)]
        loads[i].wait()
        if i >= slots:
            stores[i - slots].wait()
        obuf[i % slots] = ibuf[i].astype(F32)
        stores.append(pltpu.make_async_copy(obuf.at[i % slots], dst, osem.at[i % slots]))
        stores[-1].start()
    for cp in stores[-slots:]:
        cp.wait()


def remote(body, cid, outs, ins, scratch, name):
    def space(x):
        if x is None:
            return pl.BlockSpec(memory_space=pl.ANY)
        return pl.BlockSpec(memory_space=x)

    return pl.pallas_call(
        body,
        out_shape=[jax.ShapeDtypeStruct(s, d) for s, d, _ in outs],
        in_specs=[space(m) for _, m in ins],
        out_specs=[space(m) for _, _, m in outs],
        scratch_shapes=list(scratch),
        compiler_params=pltpu.CompilerParams(collective_id=cid, has_side_effects=True, vmem_limit_bytes=VMEM_LIMIT),
        name=name,
    )(*[x for x, _ in ins])


def local(
    inputs, cotangent, lengths, weight_noise, ffn1_in, ffn1_out, query_w, key_w, value_w, pos_w, out_w,
    conv_in, conv_out, ffn2_in, ffn2_out, conv_kernel, ffn1_gain, attn_gain, conv_gain, ffn2_gain,
    final_gain, bn_gain, bn_bias, pos_u, pos_v,
):
    _, rows, width = inputs.shape
    tms, slots = lax.axis_size("tm"), lax.axis_size("slot")
    frames = rows * tms
    count = conv_kernel.shape[0]
    devices = tms * slots
    size = Place().size
    x = inputs[0]
    cot = cotangent[0]
    gains = [g.reshape(1, -1) for g in (ffn1_gain, attn_gain, conv_gain, ffn2_gain, final_gain)]
    bng, bnb, pu, pv = (g.reshape(1, -1) for g in (bn_gain, bn_bias, pos_u, pos_v))
    raws = (ffn1_in, ffn1_out, query_w, key_w, value_w, pos_w, out_w, conv_in, conv_out, ffn2_in, ffn2_out)
    VM, HB, SM = pltpu.VMEM, None, pltpu.SMEM
    DMA = pltpu.SemaphoreType.DMA
    V = lambda shape, dtype=BF: pltpu.VMEM(shape, dtype)
    shard_rows = weight_noise.shape[1] // width
    half, hidden = width // 2, 2048
    keys = (H // 2, 2, tms, rows, LANE)
    specs = [
        ((FLAT_ROWS, width), BF), ((rows, width), F32), ((rows, hidden), F32), ((rows, width), BF), ((rows, width), BF), ((rows, width), BF),
        (keys, BF), ((frames, width), BF), ((rows, half), F32), ((rows, half), F32), ((rows, width), BF), ((H, rows, frames), BF),
    ]
    wn, x1, pre1, a2, qu, qv, kv, trig, sin, cos, att, probs = remote(
        early_body, 0, [spec + (HB,) for spec in specs],
        [(lengths, SM), (weight_noise, VM)] + [(r, HB) for r in raws] + [(x, VM), (gains[0], VM), (gains[1], VM), (pu, VM), (pv, VM)],
        [V((FLAT_ROWS, width)), V((width // LANE, shard_rows, LANE), F32)]
        + [V(*spec) for spec in specs[1:10]]
        + [V((2, frames // 64, half), F32), V((2, 64, half), F32), V((rows, width)), V((2, rows, frames)), DMA((18,)), DMA((16,)), DMA((2,))]
        + Gather.scratch(size, shard_rows, width) + KeysAll.scratch(size["x"]),
        "early",
    )
    ext = pltpu.VMEM((width // LANE, rows + count, LANE), F32)
    output, dx2, datt, g_mid, smalls2, bns, cores = remote(
        middle_body, 1,
        [((rows, width), BF, HB), ((rows, width), F32, HB), ((rows, width), BF, HB), ((3 * GROUP, width), BF, HB),
         ((count + 8, width), F32, VM), ((8, width), F32, VM), ((max(1, len(FRONT)), GROUP // 2, width), BF, HB)],
        [(lengths, SM), (att, VM), (x1, VM), (cot, VM), (wn, HB), (conv_kernel, VM), (bng, VM), (bnb, VM)] + [(g, VM) for g in gains[2:]],
        [pltpu.VMEM((FLAT_SIZE[n], width), BF) for n in ("o", "ci", "co", "f2i", "f2o")]
        + [DMA((5,)), pltpu.VMEM((count, width), BF), pltpu.VMEM((count, width), BF), DMA((4,)),
           pltpu.VMEM((rows, width), BF), pltpu.VMEM((rows, width), BF), pltpu.VMEM((rows, 2 * width), F32), ext, ext,
           pltpu.VMEM((rows, width), F32), pltpu.VMEM((rows, hidden), F32), pltpu.VMEM((rows, width), F32),
           pltpu.VMEM((count, 8, LANE), F32), pltpu.VMEM((rows, width), F32), V((max(1, len(FRONT)), GROUP // 2, width)),
           V((rows, width)), V((rows, width), F32), V((rows, width)), V((3 * GROUP, width)),
           V((rows, hidden)), V((rows, hidden)), DMA((7,))]
        + Totals.scratch(tms, slots, width) * 2 + flat_list([flat_list(flow_scratch(size, LAYOUT[n], "front")) for n in FRONT]),
        "middle",
    )
    dx0, flat, total = remote(
        late_body, 2, [((rows, width), BF, VM), ((FLAT_ROWS, width), BF, HB), ((count + 8, width), F32, VM)],
        [(t, HB) for t in (qu, qv, kv, wn, trig, sin, cos, probs, datt, att, g_mid, cores, a2, x1, dx2, x, pre1)]
        + [(smalls2, VM), (gains[1], VM), (gains[0], VM)],
        [V((rows, width)), V((rows, width)), V(keys), V((width, width)), V((frames, width)),
         V((rows, half), F32), V((rows, half), F32), V((rows, width)), V((rows, width)), V((rows, width)),
         V((rows, width), F32), V((rows, width), F32), V((rows, width)), V((3 * width, width)),
         V((3 - len(FRONT), GROUP // 2, width)), V((6, GROUP // 2, width)), DMA((H,)), DMA((20,)),
         V((rows, width)), V((width, rows)), V((width, rows)), V((width, width), F32), V((width, rows)), V((width, rows)), V((width, rows)),
         V((FLAT_ROWS // 2, width))]
        + KeyGrads.scratch(tms, rows) + Butterfly.scratch(devices, (count + 8, width))
        + flat_list([flat_list(flow_scratch(size, LAYOUT[n], "back")) for n in FRONT])
        + flat_list([flat_list(flow_scratch(size, LAYOUT[n], "whole")) for n in MID if n not in FRONT])
        + flat_list([flat_list(flow_scratch(size, LAYOUT[n], "whole")) for n in ("q", "f1i", "f1o")]),
        "late",
    )
    big = pl.pallas_call(
        widen_body,
        out_shape=[jax.ShapeDtypeStruct(r.shape, F32) for r in raws]
        + [jax.ShapeDtypeStruct((count, width), F32)] + [jax.ShapeDtypeStruct((1, width), F32)] * 9,
        in_specs=[pl.BlockSpec(memory_space=pl.ANY)] + [pl.BlockSpec(memory_space=pltpu.VMEM)] * 2,
        out_specs=[pl.BlockSpec(memory_space=pl.ANY)] * 11 + [pl.BlockSpec(memory_space=pltpu.VMEM)] * 10,
        scratch_shapes=[pltpu.VMEM((24, 512, width), BF), pltpu.VMEM((4, 512, width), F32), DMA((24,)), DMA((4,))],
        compiler_params=pltpu.CompilerParams(vmem_limit_bytes=VMEM_LIMIT),
        name="widen",
    )(flat, total, bns)
    t = [r[0] for r in big[12:]]
    return (output[None], dx0[None]) + tuple(big[:11]) + (
        big[11], t[3], t[4], t[0], t[1], t[2], t[7], t[8], t[5], t[6],
    )


def solution(mesh):
    split = P("slot", "tm", None)
    in_specs = (split, split, P("slot"), P(("tm", "slot"), None)) + (P(),) * 21
    out_specs = (split, split) + (P(),) * 21
    return jax.shard_map(local, mesh=mesh, in_specs=in_specs, out_specs=out_specs, check_vma=False)
```

profile of v0, /device:TPU:0, one launch (start us, length us, event | category | flops | bytes accessed | tf_op | source)
XLA Modules:
  0.0 316.5 jit_solution(17491405438682938029)
XLA Ops:
  1.3 106.0 %early.1 = (bf16[12288,512]{1,0:T(8,128)(2,1)}, f32[384,512]{1,0:T(8,128)}, f32[384,2048]{1,0:T(8,128)}, bf16[384,512]{1,0:T(8,128)(2,1)}, bf16[384,512]{1,0:T(8...) custom-call(s32[1]{0:T(128)S(6)} %copy.50.refs_0_.lens, ...), custom_call_target="tpu_custom_call" | custom-call | tf_op jit(solution)/shard_map/early/pallas_call | solution.py:1337
  107.3 49.1 %middle.1 = (bf16[384,512]{1,0:T(8,128)(2,1)}, f32[384,512]{1,0:T(8,128)}, bf16[384,512]{1,0:T(8,128)(2,1)}, bf16[6144,512]{1,0:T(8,128)(2,1)}, f32[40,512]{1,0:...) custom-call(s32[1]{0:T(128)S(6)} %copy.50.refs_0_.lens, bf16[384,512]{1,0:T(8,128)(2,1)} %get-tuple-element.66.att.att_h, ...), custom_call_target="tpu_custom_call" | custom-call | tf_op jit(solution)/shard_map/middle/pallas_call | solution.py:1337
  156.5 144.7 %late.1 = (bf16[384,512]{1,0:T(8,128)(2,1)}, bf16[12288,512]{1,0:T(8,128)(2,1)}, f32[40,512]{1,0:T(8,128)}) custom-call(bf16[384,512]{1,0:T(8,128)(2,1)} %get-tuple-element.70.qu_h, bf16[384,512]{1,0:T(8,128)(2,1)} %get-tuple-element.71.qv_h, bf16[4,2,4,384,128]{4,3,2,1,0:T(8,128)(2,1)} %get-tuple-element.72.kv_h, bf16[12288,512]{1,0:T(8,128)(2,1)} %get-tuple-element.68.wn, ...), custom_call_target="tpu_custom_call" | custom-call | tf_op jit(solution)/shard_map/late/pallas_call | solution.py:1337
  301.2 0.0 copy-start
  301.2 0.0 copy-start.1
  301.2 13.8 %widen.1 = (f32[512,2048]{1,0:T(8,128)}, f32[2048,512]{1,0:T(8,128)}, f32[512,512]{1,0:T(8,128)}, f32[512,512]{1,0:T(8,128)}, f32[512,512]{1,0:T(8,128)}, /*inde...) custom-call(bf16[12288,512]{1,0:T(8,128)(2,1)} %get-tuple-element.85, ...), custom_call_target="tpu_custom_call" | custom-call | tf_op jit(solution)/shard_map/widen/pallas_call | solution.py:1415
  315.0 0.0 copy-done
  315.0 0.7 copy.51
  315.8 0.0 copy-done.1
  315.8 0.7 copy.52
Async XLA Ops:
  301.2 13.8 %copy-start = (bf16[384,512]{1,0:T(8,128)(2,1)S(1)}, bf16[384,512]{1,0:T(8,128)(2,1)}, u32[]{:S(2)}) copy-start(bf16[384,512]{1,0:T(8,128)(2,1)} %get-tuple-element.69) | copy-start | bytes 1179652
  301.2 14.6 %copy-start.1 = (bf16[384,512]{1,0:T(8,128)(2,1)S(1)}, bf16[384,512]{1,0:T(8,128)(2,1)}, u32[]{:S(2)}) copy-start(bf16[384,512]{1,0:T(8,128)(2,1)} %get-tuple-element.84) | copy-start | bytes 1179652
where the time goes:
time: 318 us; the launch traced here: 317 us
  Pallas kernels  314 us (99%)
    pallas_call x3, Pallas kernels, remote(): pl.pallas_call(body, out_shape=[jax.ShapeDtypeStruct(s, d) for s, d, _ in...  300 us
    pallas_call x1, Pallas kernels, local(): pl.pallas_call(widen_body, out_shape=[jax.ShapeDtypeStruct(r.shape, F32)...  13.8 us

commit v1 on v0

--- a/solution.py
+++ b/solution.py
@@ -299,26 +299,45 @@
         flow.take()()
 
 
-EARLY = ((("y", "x", "z"), 0, 384), (("x", "y", "z"), 384, 128))
-EVEN = ((("y", "x", "z"), 0, 256), (("x", "y", "z"), 256, 256))
-
-
-ZFIRST = ((("z", "x", "y"), 0, 256), (("z", "y", "x"), 256, 256))
-LASTA = ((("y", "x", "z"), 0, 256), (("x", "y", "z"), 256, 128), (("z", "x", "y"), 384, 128))
-LASTB = ((("y", "x", "z"), 0, 128), (("x", "y", "z"), 128, 256), (("z", "y", "x"), 384, 128))
 MID = {"f2i": 2048, "f2o": 4096, "o": 0}
+NAMES = ("f2i", "f2o", "o", "q", "f1o", "f1i")
+AXES = {"A": ("y", "x", "z"), "B": ("x", "y", "z"), "X": ("z", "x", "y"), "Y": ("z", "y", "x")}
 FRONT = ("f2i",)
-LAYOUT = {"f2i": EVEN, "f2o": EVEN, "o": EVEN, "q": LASTA, "f1i": LASTB, "f1o": EVEN}
-TICKS = {0: "f2o o", 4: "f2i", 9: "f2o o", 10: "f2i", 16: "f2o o", 17: "f2i", 19: "f2o o f2i q"}
-REST = ("f2i", "f2o", "o", "q", "f1o", "f1i")
-
-
-def lanes_of(size, wanted):
-    return wanted if max(Flow.lane_parts(order, size) for order, _, _ in wanted) == 1 else EVEN
-
-
-def flow_scratch(size, layout, kind):
-    return [Flow.scratch(order, width, size, kind) for order, _, width in lanes_of(size, layout)]
+LANES = {"f2i": "A1 B3", "f2o": "A2 B1 B1", "o": "A2 B2", "q": "A2 B1 X1", "f1o": "A1 B1 A1 X1", "f1i": "B1 A1 B1 A1"}
+TURNS = {
+    -1: (4, 5, 6, 8, 9, 0, 1,),
+    0: (5, 6, 4,),
+    1: (0, 1,),
+    3: (8, 9, 0,),
+    5: (1,),
+    6: (5,),
+    7: (6,),
+    9: (5, 1, 6,),
+    12: (9, 4, 5,),
+    13: (8, 6,),
+    15: (9, 0, 5,),
+    16: (4, 1, 6,),
+    17: (8, 0, 5,),
+    18: (9,),
+    19: (12, 14, 13,),
+    20: (17, 4, 0,),
+    21: (16, 12, 13, 18, 19, 20, 8, 1, 0, 5, 14, 21, 5, 22, 17, 1, 4, 12, 20, 23, 13, 16, 18, 14, 9, 17, 22, 19, 21, 20, 8, 12, 16, 6, 4, 14, 13, 19, 23, 18, 16, 9, 8, 19, 14, 21, 6, 12, 17, 13, 22, 6, 20, 18, 4, 16, 23, 17, 21, 12, 13, 4, 19, 22, 20, 14, 18, 8, 9, 16, 23, 21, 17, 8, 9, 22, 19, 13, 20, 13, 18, 21, 23, 16, 17, 22, 16, 14, 17, 20, 23, 12, 14, 20, 19, 22, 12, 19, 18, 21, 22, 23, 18, 21, 23,),
+}
+
+
+def layout(name, size):
+    words = LANES[name].split()
+    if max(Flow.lane_parts(AXES[word[0]], size) for word in words) > 1:
+        words = ["A2", "B2"]
+    got, lane = [], 0
+    for word in words:
+        got.append((AXES[word[0]], lane, int(word[1]) * LANE))
+        lane += got[-1][2]
+    return got
+
+
+def flow_scratch(size, name, kind):
+    return [Flow.scratch(order, width, size, kind) for order, _, width in layout(name, size)]
 
 
 def flat_list(lists):
@@ -334,9 +353,9 @@
         return got
 
 
-def make_flows(pc, layout, kind, src, own, core, out, first, taker):
+def make_flows(pc, name, kind, src, own, core, out, first, taker):
     flows = []
-    for (order, lane, width), shapes in zip(lanes_of(pc.size, layout), flow_scratch(pc.size, layout, kind)):
+    for (order, lane, width), shapes in zip(layout(name, pc.size), flow_scratch(pc.size, name, kind)):
         flows.append(Flow(pc, order, lane, width, kind, src, own, core, out, first, taker(len(shapes))))
     return flows
 
@@ -358,13 +377,14 @@
     @staticmethod
     def scratch(size, shard_rows, width):
         part, pieces = Gather.cut(shard_rows)
-        links = 2 * pieces * sum(n - 1 for n in size.values())
+        links = 2 * pieces * (2 * (size["x"] + size["y"] + size["z"] - 3) + 2)
         sems = pltpu.SemaphoreType.DMA((links,))
         return [
             pltpu.VMEM((size["x"], 2, size["z"], size["y"], shard_rows, width), BF),
             pltpu.VMEM((width // LANE, 64, LANE), F32),
             sems,
             sems,
+            pltpu.SemaphoreType.REGULAR,
         ]
 
     @staticmethod
@@ -374,16 +394,18 @@
 
     def __init__(self, pc, wf, bufs):
         self.pc, self.wf = pc, wf
-        self.nb, self.scr, self.ssem, self.rsem = bufs
+        self.nb, self.scr, self.ssem, self.rsem, self.free = bufs
         self.shard_rows = self.nb.shape[4]
         self.part, self.pieces = self.cut(self.shard_rows)
         self.xs = pc.size["x"]
         self.used = 0
         self.stages = [self.plan(hx, q) for hx in range(2) for q in range(self.pieces)]
 
-    def copies(self, ref, axis):
+    def copies(self, ref, axis, only=None):
         out = []
         for off, dev, _ in self.pc.peers(axis):
+            if only is not None and off != only:
+                continue
             k = self.used
             self.used += 1
             out.append(
@@ -397,12 +419,22 @@
         pc, nb = self.pc, self.nb
         x, c, z, y = (pc.at[a] for a in "xczy")
         rows = pl.ds(q * self.part, self.part)
-        side = pl.ds(hx * (self.xs // 2), self.xs // 2)
-        in_half = lambda pos: lax.div(pos, self.xs // 2) == hx
+        across = self.xs // 2
+        side = pl.ds(hx * across, across)
+        in_half = lambda pos: lax.div(pos, across) == hx
+        width = nb.shape[5]
+        wide, quarter = pl.ds(0, width // 2), width // 4
+        away = pl.ds(3 * quarter, quarter)
+        source = jnp.where(in_half(x), x, lax.rem(x + across, self.xs))
+        lanes = pl.ds(pl.multiple_of(jnp.where(in_half(x), 2 * quarter, 3 * quarter), LANE), quarter)
         along = {
-            "x": self.copies(nb.at[x, c, z, y, rows], "x"),
-            "z": self.copies(nb.at[side, c, z, y, rows], "z"),
-            "y": self.copies(nb.at[side, c, :, y, rows], "y"),
+            "xa": self.copies(nb.at[x, c, z, y, rows, wide], "x"),
+            "xd": self.copies(nb.at[x, c, z, y, rows, away], "x", across),
+            "za": self.copies(nb.at[side, c, z, y, rows, wide], "z"),
+            "zb": self.copies(nb.at[source, c, z, y, rows, lanes], "z"),
+            "ya": self.copies(nb.at[side, c, :, y, rows, wide], "y"),
+            "yb": self.copies(nb.at[source, c, :, y, rows, lanes], "y"),
+            "xb": self.copies(nb.at[source, c, :, :, rows, lanes], "x"),
             "c": self.copies(nb.at[side, c, :, :, rows], "c"),
         }
 
@@ -424,15 +456,30 @@
                 self.mix_half(hx, None)
 
         def done():
-            each("x", "wait_send", sends)
-            for axis in "zyc":
+            each("xa", "wait_send", sends)
+            for axis in ("za", "zb", "ya", "yb", "xb", "c"):
                 each(axis, "wait_send")
 
+        def then(*acts):
+            return lambda: [each(*act) for act in acts]
+
+        def let():
+            @pl.when(in_half(x))
+            def _():
+                ((_, cp),) = along["xd"]
+                cp.wait_send()
+                ((_, dev, _),) = [peer for peer in pc.peers("x") if peer[0] == across]
+                pl.semaphore_signal(self.free, inc=1, device_id=dev, device_id_type=MESH)
+
+        def allowed():
+            pl.when(jnp.logical_not(in_half(x)))(lambda: pl.semaphore_wait(self.free, 1))
+
         return {
-            "X": lambda: each("x", "start", sends),
-            "Z": lambda: (each("x", "wait_recv", gets), each("z", "start")),
-            "Y": lambda: (each("z", "wait_recv"), each("y", "start")),
-            "C": lambda: (each("y", "wait_recv"), each("c", "start")),
+            "X": then(("xa", "start", sends), ("xd", "start", sends)),
+            "Z": then(("xa", "wait_recv", gets), ("xd", "wait_recv", gets), ("za", "start"), ("zb", "start")),
+            "Y": lambda: (then(("za", "wait_recv"), ("zb", "wait_recv"), ("ya", "start"), ("yb", "start"))(), let()),
+            "W": lambda: (each("yb", "wait_recv"), allowed(), each("xb", "start")),
+            "C": then(("ya", "wait_recv"), ("xb", "wait_recv"), ("c", "start")),
             "E": end,
             "D": done,
         }
@@ -577,8 +624,8 @@
             dst = wf.at[pl.ds(FLAT[name] + j * size, size), :]
             loads.append(pltpu.make_async_copy(raw.at[:, pl.ds(j * 512, 512)], dst, wsem.at[len(loads)]))
             loads[-1].start()
-    gather = Gather(pc, wf, bufs[:4])
-    keys = KeysAll(pc, kv, bufs[4:6])
+    gather = Gather(pc, wf, bufs[:5])
+    keys = KeysAll(pc, kv, bufs[5:7])
 
     def unfold(i, carry):
         for r in range(8):
@@ -624,9 +671,9 @@
 
     x = x_ref[...].astype(F32)
     a1 = norm(x, gain1[...]).astype(BF)
-    for t in range(2, n + 1):
-        gather.run([("Z", t), ("Y", t - 2), ("C", t - 3), ("E", t - 4)])
-    gather.run([("Y", n - 1), ("C", n - 2), ("E", n - 3), ("C", n - 1), ("E", n - 2), ("Z", n + 1), ("E", n - 1)])
+    for t in range(2, n + 2):
+        gather.run([("Z", t), ("Y", t - 2), ("W", t - 3), ("C", t - 4), ("E", t - 5)])
+    gather.run([("W", n - 1), ("C", n - 2), ("E", n - 3), ("C", n - 1), ("E", n - 2), ("Z", n + 2), ("E", n - 1)])
     part = lambda name: wf.at[pl.ds(FLAT[name], FLAT_SIZE[name]), :]
     x1 = x + 0.5 * ffn_forward(a1, part("f1i"), part("f1o"), pre_ref)
     x1_ref[...] = x1
@@ -640,7 +687,7 @@
         if p == 0:
             keys.send_line(0)
         keys.send(p)
-    gather.run([("Z", n + 2), ("Y", n)])
+    gather.run([("Z", n + 3), ("Y", n), ("Y", n + 1)])
     q = dot(a2, part("q")[...])
     scale = HD**-0.5
     qu[...] = ((q + pos_u[...]).astype(BF).astype(F32) * scale).astype(BF)
@@ -649,10 +696,11 @@
         put(src, dst)
     put(wf.at[pl.ds(0, FLAT_ROWS // 2), :], wn.at[pl.ds(0, FLAT_ROWS // 2), :])
     steps = {
-        0: "Y1 Z3", 1: "Y2 Z4 C0", 2: "C1 E0", 3: "Y3 Z5 E1", 4: "Y4 C2", 5: "C3 E2", 6: "Y5 E3", 7: "C4", 8: "C5 E4 E5",
+        0: "W0 Y2 Z4", 1: "W1 Y3 Z5", 2: "C0 W2 Y4", 3: "E0 W3 Y5", 4: "C1 W4", 5: "E1 C2 W5", 6: "E2 C3", 7: "E3 C4 C5", 8: "E4 E5",
     }
     if n != 6:
-        steps = {8: " ".join("%s%d" % (op, i) for op, low in (("Z", 3), ("Y", 1), ("C", 0), ("E", 0)) for i in range(low, n))}
+        order = (("Z", 4), ("Y", 2), ("W", 0), ("C", 0), ("E", 0))
+        steps = {8: " ".join("%s%d" % (op, i) for op, low in order for i in range(low, n))}
     steps = {at: [(op[0], n + int(op[1:])) for op in text.split()] for at, text in steps.items()}
     plan = {at: (lambda ops=ops: gather.run(ops)) for at, ops in steps.items() if at < H}
     ok = lax.broadcasted_iota(jnp.int32, (1, frames), 1) < lens[0]
@@ -666,19 +714,17 @@
             mine = lane_half(e)
             qve = jnp.where(mine, qv[:, at], jnp.zeros((), BF))
             que = jnp.where(mine, qu[:, at], jnp.zeros((), BF))
-            a_s = dot_nt(qve, w_pos[pl.ds(0, half), at])
-            a_c = dot_nt(qve, w_pos[pl.ds(half, half), at])
+            turned = dot_nt(qve, w_pos[:, at])
+            a_s, a_c = turned[:, :half], turned[:, half:]
             b_c = (a_s * sin[...] + a_c * cos[...]).astype(BF)
             b_s = (a_c * sin[...] - a_s * cos[...]).astype(BF)
             if e == 0:
                 pl.when(p == 1)(lambda: keys.send_line(3))
+                pl.when(p == 0)(lambda: (keys.forward(0), keys.send_line(1))[1])
+                keys.ready(p)
             else:
                 pl.when(p == 0)(lambda: keys.send_line(2))
-            s = dot_nt(b_s, trig[:, pl.ds(0, half)]) + dot_nt(b_c, trig[:, pl.ds(half, half)])
-            if e == 0:
-                pl.when(p == 0)(lambda: (keys.forward(0), keys.send_line(1))[1])
-                keys.ready(p)
-            s = s + dot_nt(que, kv[p, 0].reshape(frames, LANE))
+            s = dot_nt(jnp.concatenate([b_s, b_c, que], axis=1), jnp.concatenate([trig[...], kv[p, 0].reshape(frames, LANE)], axis=1))
             s = jnp.where(ok, s, FILL)
             m = jnp.max(s, axis=-1, keepdims=True)
             ex = jnp.exp(s - m)
@@ -892,7 +938,7 @@
     for i, name in enumerate(FRONT):
         src = g_ref.at[pl.ds(MID[name], GROUP), :]
         half_rows = lambda o, n, lanes, src=src: src[pl.ds(pl.multiple_of(pc.at["c"] * (GROUP // 2) + o, 16), n), lanes]
-        flows += make_flows(pc, LAYOUT[name], "front", src, half_rows, core.at[i], None, 0, taker)
+        flows += make_flows(pc, name, "front", src, half_rows, core.at[i], None, 0, taker)
 
     def halo(src, dst, k, step):
         dev = (lax.rem(pc.tm + step + tms, tms), pc.slot)
@@ -1155,31 +1201,31 @@
     fly = Butterfly(pc, total_ref, taker(3))
     groups = {}
     for i, name in enumerate(FRONT):
-        groups[name] = make_flows(pc, LAYOUT[name], "back", None, None, core.at[i], flat, FLAT[name], taker)
+        groups[name] = make_flows(pc, name, "back", None, None, core.at[i], flat, FLAT[name], taker)
     for i, name in enumerate(whole):
         mine = lambda o, n, lanes, i=i: own[i, pl.ds(o, n), lanes]
         src = g_mid.at[pl.ds(MID[name], GROUP), :]
-        groups[name] = make_flows(pc, LAYOUT[name], "whole", src, mine, core.at[len(FRONT) + i], flat, FLAT[name], taker)
+        groups[name] = make_flows(pc, name, "whole", src, mine, core.at[len(FRONT) + i], flat, FLAT[name], taker)
     for i, name in enumerate(("q", "f1i", "f1o")):
         at = FLAT[name]
         mine = lambda o, n, lanes, at=at: g_low[pl.ds(pl.multiple_of(at + c * (GROUP // 2) + o, 16), n), lanes]
-        groups[name] = make_flows(pc, LAYOUT[name], "whole", g_low.at[pl.ds(at, GROUP), :], mine, core.at[3 + i], flat, at, taker)
+        groups[name] = make_flows(pc, name, "whole", g_low.at[pl.ds(at, GROUP), :], mine, core.at[3 + i], flat, at, taker)
     for cp in owns:
         cp.wait()
-    for name in MID:
-        advance(groups[name])
+    def run(point):
+        picked = [(NAMES[token // 4], token % 4) for token in TURNS.get(point, ())]
+        stages = [groups[name][i].take() for name, i in picked if i < len(groups[name])]
+        return lambda: [stage() for stage in stages]
+
+    run(-1)()
     for cp in early:
         cp.wait()
     qut[...] = qu[...].T
     qvt[...] = qv[...].T
     datt_t[...] = datt[...].T
 
-    def run(members):
-        stages = [flow.take() for name in members.split() for flow in groups[name]]
-        return lambda: [stage() for stage in stages]
-
-    plan = {at: run(members) for at, members in sorted(TICKS.items()) if at < 2 * H}
-    after = lambda point: run(TICKS.get(point, ""))()
+    plan = {at: run(at) for at in range(2 * H)}
+    after = lambda point: run(point)()
     scale = HD**-0.5
 
     def scores(p, pbuf, load):
@@ -1209,14 +1255,13 @@
             mine = lane_half(e)
             part = pl.ds(pl.multiple_of(p * LANE + e * HD, HD), HD)
             ds = pbuf[2 * p + e]
-            db_s = dot(ds, trig[:, pl.ds(0, half)])
-            db_c = dot(ds, trig[:, pl.ds(half, half)])
+            back = dot(ds, jnp.concatenate([trig[...], kv[p, 0].reshape(-1, LANE)], axis=1))
+            db_s, db_c, part_u = back[:, :half], back[:, half : 2 * half], back[:, 2 * half :]
             da_s = (db_c * sin[...] - db_s * cos[...]).astype(BF)
             da_c = (db_c * cos[...] + db_s * sin[...]).astype(BF)
-            gpost[part, pl.ds(0, half)] = dot(qvt[part, :], da_s)
-            gpost[part, pl.ds(half, half)] = dot(qvt[part, :], da_c)
-            part_v = dot(da_s, w_p[pl.ds(0, half), at]) + dot(da_c, w_p[pl.ds(half, half), at])
-            part_u = dot(ds, kv[p, 0].reshape(-1, LANE))
+            turned = jnp.concatenate([da_s, da_c], axis=1)
+            gpost[part, :] = dot(qvt[part, :], turned)
+            part_v = dot(turned, w_p[:, at])
             dqu = part_u if e == 0 else jnp.where(mine, part_u, dqu)
             dqv = part_v if e == 0 else jnp.where(mine, part_v, dqv)
             if e == 0:
@@ -1255,10 +1300,10 @@
         g_low[pl.ds(FLAT["k"], 512), :] = dot_nt(a2t, dkt[...]).astype(BF)
         g_low[pl.ds(FLAT["v"], 512), :] = dot_nt(a2t, dvt[...]).astype(BF)
         advance(groups["q"])
-        after(17)
         for cp in last_in:
             cp.wait()
         ffn_hidden(pre_ref, hid_ref)
+        after(17)
         da2 = da2 + dot_nt(dkt[...].T, wqkv[pl.ds(512, 512), :]) + dot_nt(dvt[...].T, wqkv[pl.ds(1024, 512), :])
         back, gg2 = norm_back(x1_ref[...], gain2[...], da2)
         dx1 = dx2_ref[...] + back
@@ -1268,10 +1313,11 @@
         after(18)
         ffn_out_grad(g1, hid_ref, g_low.at[pl.ds(2048, 2048), :])
         advance(groups["f1o"])
+        after(19)
         da1 = ffn_through(g1, w1.at[pl.ds(0, 2048), :], w1.at[pl.ds(2048, 2048), :], pre_ref, hid_ref, dpre_ref)
+        after(20)
         ffn_in_grad(a1, dpre_ref, g_low.at[pl.ds(0, 2048), :])
         advance(groups["f1i"])
-        after(19)
         back, gg1 = norm_back(x, gain1[...], da1)
         dx0_ref[...] = (dx1 + back).astype(BF)
         total_ref[pl.ds(smalls2.shape[0] - 5, 2), :] = jnp.concatenate([gg1, gg2], axis=0)
@@ -1282,12 +1328,14 @@
     total_ref[pl.ds(count, 3), :] = smalls2[pl.ds(count, 3), :]
     total_ref[pl.ds(count + 7, 1), :] = jnp.zeros((1, 512), F32)
     flows = flat_list(list(groups.values()))
-    t = 0
-    while any(flow.now < flow.last for flow in flows) or t <= len(fly.devs):
-        advance([flow for i in range(4) for name in REST if i < len(groups[name]) for flow in groups[name][i : i + 1]])
-        if t <= len(fly.devs):
-            fly.stage(t)
-        t += 1
+    turns, steps = TURNS[21], len(fly.devs) + 1
+    for i, token in enumerate(turns):
+        if i * steps // len(turns) != (i - 1) * steps // len(turns):
+            fly.stage(i * steps // len(turns))
+        name, k = NAMES[token // 4], token % 4
+        advance(groups[name][k : k + 1])
+    while any(flow.now < flow.last for flow in flows):
+        advance(flows)
     for p in range(H // 2):
         keys.sent(p)
     for flow in flows:
@@ -1393,7 +1441,7 @@
            pltpu.VMEM((count, 8, LANE), F32), pltpu.VMEM((rows, width), F32), V((max(1, len(FRONT)), GROUP // 2, width)),
            V((rows, width)), V((rows, width), F32), V((rows, width)), V((3 * GROUP, width)),
            V((rows, hidden)), V((rows, hidden)), DMA((7,))]
-        + Totals.scratch(tms, slots, width) * 2 + flat_list([flat_list(flow_scratch(size, LAYOUT[n], "front")) for n in FRONT]),
+        + Totals.scratch(tms, slots, width) * 2 + flat_list([flat_list(flow_scratch(size, n, "front")) for n in FRONT]),
         "middle",
     )
     dx0, flat, total = remote(
@@ -1407,9 +1455,9 @@
          V((rows, width)), V((width, rows)), V((width, rows)), V((width, width), F32), V((width, rows)), V((width, rows)), V((width, rows)),
          V((FLAT_ROWS // 2, width))]
         + KeyGrads.scratch(tms, rows) + Butterfly.scratch(devices, (count + 8, width))
-        + flat_list([flat_list(flow_scratch(size, LAYOUT[n], "back")) for n in FRONT])
-        + flat_list([flat_list(flow_scratch(size, LAYOUT[n], "whole")) for n in MID if n not in FRONT])
-        + flat_list([flat_list(flow_scratch(size, LAYOUT[n], "whole")) for n in ("q", "f1i", "f1o")]),
+        + flat_list([flat_list(flow_scratch(size, n, "back")) for n in FRONT])
+        + flat_list([flat_list(flow_scratch(size, n, "whole")) for n in MID if n not in FRONT])
+        + flat_list([flat_list(flow_scratch(size, n, "whole")) for n in ("q", "f1i", "f1o")]),
         "late",
     )
     big = pl.pallas_call(

time: 318 us -> 295 us (0.928)
  Pallas kernels: 314 us -> 291 us
    pallas_call x3, Pallas kernels: 300 us -> 277 us  [remote(): pl.pallas_call(body, out_shape=[jax.ShapeDtypeStruct(s, d) for s, d, _ in...]
where the time goes in v1:
time: 295 us; the launch traced here: 294 us
  Pallas kernels  291 us (99%)
    pallas_call x3, Pallas kernels, remote(): pl.pallas_call(body, out_shape=[jax.ShapeDtypeStruct(s, d) for s, d, _ in...  277 us
    pallas_call x1, Pallas kernels, local(): pl.pallas_call(widen_body, out_shape=[jax.ShapeDtypeStruct(r.shape, F32)...  13.8 us

profile of v1, /device:TPU:0, one launch (start us, length us, event | category | flops | bytes accessed | tf_op | source)
XLA Modules:
  0.0 294.2 jit_solution(8979274161485947270)
XLA Ops:
  1.3 100.8 %early.1 = (bf16[12288,512]{1,0:T(8,128)(2,1)}, f32[384,512]{1,0:T(8,128)}, f32[384,2048]{1,0:T(8,128)}, bf16[384,512]{1,0:T(8,128)(2,1)}, bf16[384,512]{1,0:T(8...) custom-call(s32[1]{0:T(128)S(6)} %copy.50.refs_0_.lens, ...), custom_call_target="tpu_custom_call" | custom-call | tf_op jit(solution)/shard_map/early/pallas_call | solution.py:1385
  102.2 48.0 %middle.1 = (bf16[384,512]{1,0:T(8,128)(2,1)}, f32[384,512]{1,0:T(8,128)}, bf16[384,512]{1,0:T(8,128)(2,1)}, bf16[6144,512]{1,0:T(8,128)(2,1)}, f32[40,512]{1,0:...) custom-call(s32[1]{0:T(128)S(6)} %copy.50.refs_0_.lens, bf16[384,512]{1,0:T(8,128)(2,1)} %get-tuple-element.66.att.att_h, ...), custom_call_target="tpu_custom_call" | custom-call | tf_op jit(solution)/shard_map/middle/pallas_call | solution.py:1385
  150.2 128.7 %late.1 = (bf16[384,512]{1,0:T(8,128)(2,1)}, bf16[12288,512]{1,0:T(8,128)(2,1)}, f32[40,512]{1,0:T(8,128)}) custom-call(bf16[384,512]{1,0:T(8,128)(2,1)} %get-tuple-element.70.qu_h, bf16[384,512]{1,0:T(8,128)(2,1)} %get-tuple-element.71.qv_h, bf16[4,2,4,384,128]{4,3,2,1,0:T(8,128)(2,1)} %get-tuple-element.72.kv_h, bf16[12288,512]{1,0:T(8,128)(2,1)} %get-tuple-element.68.wn, ...), custom_call_target="tpu_custom_call" | custom-call | tf_op jit(solution)/shard_map/late/pallas_call | solution.py:1385
  278.8 0.0 copy-start
  278.8 0.0 copy-start.1
  278.9 13.8 %widen.1 = (f32[512,2048]{1,0:T(8,128)}, f32[2048,512]{1,0:T(8,128)}, f32[512,512]{1,0:T(8,128)}, f32[512,512]{1,0:T(8,128)}, f32[512,512]{1,0:T(8,128)}, /*inde...) custom-call(bf16[12288,512]{1,0:T(8,128)(2,1)} %get-tuple-element.85, ...), custom_call_target="tpu_custom_call" | custom-call | tf_op jit(solution)/shard_map/widen/pallas_call | solution.py:1463
  292.7 0.0 copy-done
  292.7 0.7 copy.51
  293.4 0.0 copy-done.1
  293.4 0.7 copy.52
Async XLA Ops:
  278.8 13.8 %copy-start = (bf16[384,512]{1,0:T(8,128)(2,1)S(1)}, bf16[384,512]{1,0:T(8,128)(2,1)}, u32[]{:S(2)}) copy-start(bf16[384,512]{1,0:T(8,128)(2,1)} %get-tuple-element.69) | copy-start | bytes 1179652
  278.8 14.6 %copy-start.1 = (bf16[384,512]{1,0:T(8,128)(2,1)S(1)}, bf16[384,512]{1,0:T(8,128)(2,1)}, u32[]{:S(2)}) copy-start(bf16[384,512]{1,0:T(8,128)(2,1)} %get-tuple-element.84) | copy-start | bytes 1179652

commit v2 on v1

--- a/solution.py
+++ b/solution.py
@@ -113,7 +113,7 @@
             for _, dev, _ in self.peers(axis):
                 pl.semaphore_signal(bar, inc=1, device_id=dev, device_id_type=MESH)
                 count += 1
-        pl.semaphore_wait(bar, count)
+        return lambda: pl.semaphore_wait(bar, count)
 
 
 def rows_at(start, size):
@@ -149,7 +149,7 @@
 
     @staticmethod
     def scratch(order, width, size, kind):
-        shapes, sends = [], 2
+        shapes = []
         blk = GROUP // 2
         parts = Flow.lane_parts(order, size)
         for lv, axis in enumerate(order):
@@ -158,17 +158,15 @@
             w = width // parts if lv == 2 else width
             if (kind != "front" or lv == 0) and (kind != "back" or lv > 0):
                 shapes.append(pltpu.VMEM((n - 1, blk, w), BF))
-            sends += 2 * (n - 1)
         if kind != "front":
             shapes.append(pltpu.VMEM((blk, width // parts), BF))
-        sems = pltpu.SemaphoreType.DMA((sends,))
-        return shapes + [sems, sems, pltpu.SemaphoreType.DMA((1,))]
+        sems = pltpu.SemaphoreType.DMA
+        return shapes + [sems((3,)), sems((2,)) if kind == "front" else sems((8,)), sems((1,))]
 
     def __init__(self, pc, order, lane, width, kind, src, own, core, out, first, bufs):
         self.ssem, self.rsem, self.lsem = bufs[-3:]
         bufs = list(bufs[:-3])
-        self.used, self.now = 0, 2 if kind == "back" else 0
-        self.made, self.local = [], []
+        self.now = 2 if kind == "back" else 0
         size = pc.size
         lanes = pl.ds(lane, width)
         c = pc.at["c"]
@@ -193,8 +191,8 @@
             into[0] = bufs.pop(0)
         if kind != "front":
             into[1], into[2], fin = bufs
-        core_copy = [self.copy(lambda: src.at[rows_at((1 - c) * top, top), lanes], lambda: core.at[:, lanes], cdev)]
-        down = []
+        copies = [[(lambda: src.at[rows_at((1 - c) * top, top), lanes], lambda: core.at[:, lanes], cdev)]]
+        bytes_of = [lambda: core.at[:, lanes]]
         for lv, axis in enumerate(order):
             cps = []
             for off, dev, pos in pc.peers(axis):
@@ -202,15 +200,24 @@
                     s = lambda lv=lv, pos=pos: core.at[rows_at(rel[lv] + pos * blk[lv + 1], blk[lv + 1]), lanes]
                 else:
                     s = lambda pos=pos: core.at[rows_at(share(pos)[0], low), share(pos)[1]]
-                cps.append(self.copy(s, lambda lv=lv, off=off: into[lv].at[off - 1], dev))
-            down.append(cps)
+                cps.append((s, lambda lv=lv, off=off: into[lv].at[off - 1], dev))
+            copies.append(cps)
+            bytes_of.append(lambda lv=lv: into[lv])
         mine = share(pc.at[order[2]])
         out_share = lambda: out.at[rows_at(first + c * top + mine[0], low), mine[1]]
         out_at = lambda lv: out.at[rows_at(first + c * top + rel[lv], blk[lv]), lanes]
-        up = [[self.copy(lambda: fin, out_share, dev) for _, dev, _ in pc.peers(order[2])]]
+        copies.append([(lambda: fin, out_share, dev) for _, dev, _ in pc.peers(order[2])])
+        bytes_of.append(
+            lambda: out.at[rows_at(first + c * top + rel[2], (size[order[2]] - 1) * low), pl.ds(lane, width // parts)]
+        )
         for lv in (2, 1):
-            up.append([self.copy(lambda lv=lv: out_at(lv), lambda lv=lv: out_at(lv), dev) for _, dev, _ in pc.peers(order[lv - 1])])
-        up.append([self.copy(lambda: out_at(0), lambda: out_at(0), cdev)])
+            copies.append([(lambda lv=lv: out_at(lv), lambda lv=lv: out_at(lv), dev) for _, dev, _ in pc.peers(order[lv - 1])])
+            bytes_of.append(
+                lambda lv=lv: out.at[rows_at(first + c * top + rel[lv - 1], (size[order[lv - 1]] - 1) * blk[lv]), lanes]
+            )
+        copies.append([(lambda: out_at(0), lambda: out_at(0), cdev)])
+        bytes_of.append(lambda: out_at(0))
+        self.copies, self.bytes_of = copies, bytes_of
 
         def fold(lv):
             if lv == 0:
@@ -228,70 +235,77 @@
         keep = lambda: pltpu.make_async_copy(fin, out_share(), self.lsem.at[0])
 
         def s1():
-            self.arrived(core_copy)
+            self.arrived(0)
             fold(0)
-            self.start(down[0])
+            self.start(1)
 
         def s2():
             if kind != "back":
-                self.arrived(down[0])
+                self.arrived(1)
                 fold(1)
             if kind != "front":
-                self.start(down[1])
+                self.start(2)
 
         def s3():
-            self.arrived(down[1])
+            self.arrived(2)
             fold(2)
-            self.start(down[2])
+            self.start(3)
 
         def s4():
-            self.arrived(down[2])
+            self.arrived(3)
             fold(3)
             keep().start()
-            self.start(up[0])
+            self.start(4)
 
         def climb(i):
             def run():
                 if i == 0:
                     keep().wait()
-                self.arrived(up[i])
+                self.arrived(4 + i)
                 if i < 3:
-                    self.start(up[i + 1])
+                    self.start(5 + i)
 
             return run
 
-        self.stages = [lambda: self.start(core_copy), s1, s2, s3, s4] + [climb(i) for i in range(4)]
+        self.stages = [lambda: self.start(0), s1, s2, s3, s4] + [climb(i) for i in range(4)]
         self.last = 3 if kind == "front" else self.STAGES
-        self.sent = {"front": core_copy + down[0], "back": down[1] + down[2] + sum(up, []), "whole": core_copy + sum(down + up, [])}[kind]
-
-    def copy(self, src, dst, dev):
-        k = self.used
-        self.used += 1
-        return src, dst, k, dev
-
-    def make(self, cp):
-        src, dst, k, dev = cp
+        self.first = 2 if kind == "back" else 0
+
+    def make(self, i, src, dst, dev):
         return pltpu.make_async_remote_copy(
-            src_ref=src(), dst_ref=dst(), send_sem=self.ssem.at[k], recv_sem=self.rsem.at[k], device_id=dev, device_id_type=MESH
+            src_ref=src(), dst_ref=dst(), send_sem=self.ssem.at[i % 3], recv_sem=self.rsem.at[i], device_id=dev, device_id_type=MESH
         )
 
-    def start(self, cps):
-        for cp in cps:
-            self.make(cp).start()
-
-    def arrived(self, cps):
-        for cp in cps:
-            self.make(cp).wait_recv()
+    def start(self, i):
+        for src, dst, dev in self.copies[i]:
+            self.make(i, src, dst, dev).start()
+
+    def all_of(self, i):
+        if len(self.copies[i]) == 1:
+            return self.make(i, *self.copies[i][0])
+        return self.make(i, self.bytes_of[i], self.bytes_of[i], self.copies[i][0][2])
+
+    def arrived(self, i):
+        self.all_of(i).wait_recv()
+
+    def left(self, i):
+        if i >= self.first:
+            self.all_of(i).wait_send()
 
     def finish(self):
-        for cp in self.sent:
-            self.make(cp).wait_send()
+        self.left(self.last - 2)
 
     def take(self):
         if self.now >= self.last:
             return lambda: None
-        self.now += 1
-        return self.stages[self.now - 1]
+        i, self.now = self.now, self.now + 1
+
+        def run():
+            self.stages[i]()
+            if i > 1:
+                self.left(i - 2)
+
+        return run
 
 
 def advance(flows):
@@ -303,25 +317,27 @@
 NAMES = ("f2i", "f2o", "o", "q", "f1o", "f1i")
 AXES = {"A": ("y", "x", "z"), "B": ("x", "y", "z"), "X": ("z", "x", "y"), "Y": ("z", "y", "x")}
 FRONT = ("f2i",)
-LANES = {"f2i": "A1 B3", "f2o": "A2 B1 B1", "o": "A2 B2", "q": "A2 B1 X1", "f1o": "A1 B1 A1 X1", "f1i": "B1 A1 B1 A1"}
+LANES = {"f2i": "A2 B2", "f2o": "B1 A1 B1 A1", "o": "A1 B1 A1 B1", "q": "A1 B1 A1 X1", "f1o": "A2 B1 X1", "f1i": "A1 B2 Y1"}
 TURNS = {
-    -1: (4, 5, 6, 8, 9, 0, 1,),
-    0: (5, 6, 4,),
-    1: (0, 1,),
-    3: (8, 9, 0,),
-    5: (1,),
-    6: (5,),
-    7: (6,),
-    9: (5, 1, 6,),
-    12: (9, 4, 5,),
-    13: (8, 6,),
-    15: (9, 0, 5,),
-    16: (4, 1, 6,),
-    17: (8, 0, 5,),
-    18: (9,),
-    19: (12, 14, 13,),
-    20: (17, 4, 0,),
-    21: (16, 12, 13, 18, 19, 20, 8, 1, 0, 5, 14, 21, 5, 22, 17, 1, 4, 12, 20, 23, 13, 16, 18, 14, 9, 17, 22, 19, 21, 20, 8, 12, 16, 6, 4, 14, 13, 19, 23, 18, 16, 9, 8, 19, 14, 21, 6, 12, 17, 13, 22, 6, 20, 18, 4, 16, 23, 17, 21, 12, 13, 4, 19, 22, 20, 14, 18, 8, 9, 16, 23, 21, 17, 8, 9, 22, 19, 13, 20, 13, 18, 21, 23, 16, 17, 22, 16, 14, 17, 20, 23, 12, 14, 20, 19, 22, 12, 19, 18, 21, 22, 23, 18, 21, 23,),
+    -1: (4, 5, 6, 7, 8, 9, 10, 11, 0, 1,),
+    0: (4, 5, 6,),
+    1: (8, 0, 10,),
+    2: (1, 7,),
+    3: (9,),
+    4: (0, 4,),
+    5: (6, 1,),
+    8: (4, 9, 6,),
+    9: (1,),
+    11: (9, 4, 8,),
+    12: (6,),
+    13: (5, 0,),
+    15: (8, 4, 10,),
+    16: (5, 11, 9,),
+    17: (8, 0, 4,),
+    18: (12, 5, 13,),
+    19: (14, 8, 15,),
+    20: (16, 17, 18,),
+    21: (12, 13, 10, 7, 0, 4, 14, 22, 20, 5, 4, 12, 21, 13, 17, 10, 18, 7, 0, 14, 16, 8, 11, 17, 12, 18, 9, 20, 5, 11, 13, 18, 16, 15, 1, 8, 14, 6, 7, 10, 8, 21, 20, 15, 17, 12, 5, 22, 15, 5, 11, 10, 13, 9, 21, 22, 12, 14, 20, 1, 17, 13, 16, 22, 10, 9, 18, 1, 11, 21, 14, 20, 10, 9, 22, 12, 17, 18, 16, 12, 13, 20, 22, 21, 13, 14, 6, 14, 7, 17, 16, 17, 15, 18, 20, 11, 21, 7, 18, 20, 6, 22, 15, 6, 22, 11, 16, 7, 11, 15, 21, 7, 16, 15, 21,),
 }
 
 
@@ -377,8 +393,7 @@
     @staticmethod
     def scratch(size, shard_rows, width):
         part, pieces = Gather.cut(shard_rows)
-        links = 2 * pieces * (2 * (size["x"] + size["y"] + size["z"] - 3) + 2)
-        sems = pltpu.SemaphoreType.DMA((links,))
+        sems = pltpu.SemaphoreType.DMA((2 * pieces * (size["x"] + 6),))
         return [
             pltpu.VMEM((size["x"], 2, size["z"], size["y"], shard_rows, width), BF),
             pltpu.VMEM((width // LANE, 64, LANE), F32),
@@ -401,19 +416,24 @@
         self.used = 0
         self.stages = [self.plan(hx, q) for hx in range(2) for q in range(self.pieces)]
 
-    def copies(self, ref, axis, only=None):
+    def copies(self, ref, axis, only=None, total=None):
         out = []
+
+        def make(ref, dev, k):
+            return pltpu.make_async_remote_copy(
+                src_ref=ref, dst_ref=ref, send_sem=self.ssem.at[k], recv_sem=self.rsem.at[k], device_id=dev, device_id_type=MESH
+            )
+
         for off, dev, _ in self.pc.peers(axis):
             if only is not None and off != only:
                 continue
-            k = self.used
-            self.used += 1
-            out.append(
-                (off, pltpu.make_async_remote_copy(
-                    src_ref=ref, dst_ref=ref, send_sem=self.ssem.at[k], recv_sem=self.rsem.at[k], device_id=dev, device_id_type=MESH
-                ))
-            )
-        return out
+            out.append((off, make(ref, dev, self.used)))
+            if total is None:
+                self.used += 1
+        if total is None:
+            return out, out
+        self.used += 1
+        return out, [(0, make(total, dev, self.used - 1))]
 
     def plan(self, hx, q):
         pc, nb = self.pc, self.nb
@@ -427,19 +447,20 @@
         away = pl.ds(3 * quarter, quarter)
         source = jnp.where(in_half(x), x, lax.rem(x + across, self.xs))
         lanes = pl.ds(pl.multiple_of(jnp.where(in_half(x), 2 * quarter, 3 * quarter), LANE), quarter)
+        others = {axis: pl.ds(0, pc.size[axis] - 1) for axis in "xyz"}
         along = {
             "xa": self.copies(nb.at[x, c, z, y, rows, wide], "x"),
             "xd": self.copies(nb.at[x, c, z, y, rows, away], "x", across),
-            "za": self.copies(nb.at[side, c, z, y, rows, wide], "z"),
-            "zb": self.copies(nb.at[source, c, z, y, rows, lanes], "z"),
-            "ya": self.copies(nb.at[side, c, :, y, rows, wide], "y"),
-            "yb": self.copies(nb.at[source, c, :, y, rows, lanes], "y"),
-            "xb": self.copies(nb.at[source, c, :, :, rows, lanes], "x"),
+            "za": self.copies(nb.at[side, c, z, y, rows, wide], "z", None, nb.at[side, c, others["z"], y, rows, wide]),
+            "zb": self.copies(nb.at[source, c, z, y, rows, lanes], "z", None, nb.at[source, c, others["z"], y, rows, lanes]),
+            "ya": self.copies(nb.at[side, c, :, y, rows, wide], "y", None, nb.at[side, c, :, others["y"], rows, wide]),
+            "yb": self.copies(nb.at[source, c, :, y, rows, lanes], "y", None, nb.at[source, c, :, others["y"], rows, lanes]),
+            "xb": self.copies(nb.at[source, c, :, :, rows, lanes], "x", None, nb.at[others["x"], c, :, :, rows, lanes]),
             "c": self.copies(nb.at[side, c, :, :, rows], "c"),
         }
 
         def each(axis, what, cond=None):
-            for off, cp in along[axis]:
+            for off, cp in along[axis][0 if what == "start" else 1]:
                 if cond is None:
                     getattr(cp, what)()
                 else:
@@ -450,15 +471,16 @@
 
         def end():
             each("c", "wait_recv")
+            each("xa", "wait_send", sends)
+            for axis in ("za", "zb", "ya", "yb", "xb"):
+                each(axis, "wait_send")
             if self.part == 64:
                 self.mix_half(hx, q)
             elif q == self.pieces - 1:
                 self.mix_half(hx, None)
 
         def done():
-            each("xa", "wait_send", sends)
-            for axis in ("za", "zb", "ya", "yb", "xb", "c"):
-                each(axis, "wait_send")
+            each("c", "wait_send")
 
         def then(*acts):
             return lambda: [each(*act) for act in acts]
@@ -466,7 +488,7 @@
         def let():
             @pl.when(in_half(x))
             def _():
-                ((_, cp),) = along["xd"]
+                ((_, cp),) = along["xd"][0]
                 cp.wait_send()
                 ((_, dev, _),) = [peer for peer in pc.peers("x") if peer[0] == across]
                 pl.semaphore_signal(self.free, inc=1, device_id=dev, device_id_type=MESH)
@@ -617,6 +639,7 @@
     half = width // 2
     tms = lax.axis_size("tm")
     frames = rows * tms
+    met = pc.greet("cxyz")
     loads = []
     for name, raw in zip(ORDER, raws):
         for j in range(FOLDS.get(name, 1)):
@@ -638,10 +661,6 @@
     lax.fori_loop(0, shard_rows // 8, unfold, 0)
     for b in range(width // LANE):
         gather.nb[pc.at["x"], pc.at["c"], pc.at["z"], pc.at["y"], :, pl.ds(b * LANE, LANE)] = flat[b].astype(BF)
-    pc.greet("cxyz")
-    n = gather.pieces
-    gather.run([("X", i) for i in range(2 * n)])
-    gather.run([("Z", 0), ("Z", 1)])
     rates = jnp.exp(lax.broadcasted_iota(jnp.int32, (1, half), 1).astype(F32) * (-2.0 * math.log(10000.0) / width))
     angle_tables(hi, lo, rates)
 
@@ -660,6 +679,10 @@
 
     lax.fori_loop(0, frames // 64, angles, 0)
     lax.fori_loop(0, rows // 64, own_angles, 0)
+    met()
+    n = gather.pieces
+    gather.run([("X", i) for i in range(2 * n)])
+    gather.run([("Z", 0), ("Z", 1)])
     for cp in loads:
         cp.wait()
     outs = []
@@ -1158,12 +1181,14 @@
         if i == 3:
             for cp in self.third(p):
                 cp.wait_recv()
+            for cp in self.first(p) + self.second(p):
+                cp.wait_send()
             return
         for cp in (self.first, self.second, self.third)[i](p):
             cp.start()
 
     def sent(self, p):
-        for cp in self.first(p) + self.second(p) + self.third(p):
+        for cp in self.third(p):
             cp.wait_send()
 
     def collect(self, p, kind, dst):
@@ -1186,16 +1211,19 @@
     fetch = Fetch(fsem)
     c = pc.at["c"]
     whole = [name for name in MID if name not in FRONT]
+    met = pc.greet("cxyz")
     owns = [fetch(g_mid.at[rows_at(MID[name] + c * (GROUP // 2), GROUP // 2), :], own.at[i]) for i, name in enumerate(whole)]
     owns += [fetch(cores_h.at[i], core.at[i]) for i in range(len(FRONT))]
-    early = [fetch(s, d) for s, d in ((qu_h, qu), (qv_h, qv), (datt_h, datt), (kv_h, kv), (att_h, att), (part_of(wn, "p"), w_p), (trig_h, trig), (sin_h, sin), (cos_h, cos))]
-    later = [
-        fetch(s, d)
-        for s, d in (
-            (a2_h, a2), (x1_h, x1_ref), (dx2_h, dx2_ref), (x_h, x_ref), (wn.at[pl.ds(FLAT["q"], 1536), :], wqkv),
-        )
-    ]
-    pc.greet("cxyz")
+    needed = [fetch(s, d) for s, d in ((qu_h, qu), (datt_h, datt), (att_h, att), (kv_h, kv))]
+
+    def copies(first, pairs):
+        return lambda: [pltpu.make_async_copy(s, d, fsem.at[first + i]) for i, (s, d) in enumerate(pairs)]
+
+    second = copies(fetch.n, ((qv_h, qv), (part_of(wn, "p"), w_p), (trig_h, trig), (sin_h, sin), (cos_h, cos)))
+    later = copies(
+        fetch.n + 5, ((a2_h, a2), (x1_h, x1_ref), (dx2_h, dx2_ref), (x_h, x_ref), (wn.at[pl.ds(FLAT["q"], 1536), :], wqkv))
+    )
+    last_in = lambda pre_ref, w1: copies(fetch.n + 10, ((pre_h, pre_ref), (wn.at[pl.ds(0, 4096), :], w1)))()
     taker = Taker(bufs)
     keys = KeyGrads(pc, taker(7))
     fly = Butterfly(pc, total_ref, taker(3))
@@ -1210,20 +1238,12 @@
         at = FLAT[name]
         mine = lambda o, n, lanes, at=at: g_low[pl.ds(pl.multiple_of(at + c * (GROUP // 2) + o, 16), n), lanes]
         groups[name] = make_flows(pc, name, "whole", g_low.at[pl.ds(at, GROUP), :], mine, core.at[3 + i], flat, at, taker)
-    for cp in owns:
-        cp.wait()
     def run(point):
         picked = [(NAMES[token // 4], token % 4) for token in TURNS.get(point, ())]
         stages = [groups[name][i].take() for name, i in picked if i < len(groups[name])]
         return lambda: [stage() for stage in stages]
 
-    run(-1)()
-    for cp in early:
-        cp.wait()
-    qut[...] = qu[...].T
-    qvt[...] = qv[...].T
-    datt_t[...] = datt[...].T
-
+    first = run(-1)
     plan = {at: run(at) for at in range(2 * H)}
     after = lambda point: run(point)()
     scale = HD**-0.5
@@ -1275,19 +1295,36 @@
         total_ref[pl.ds(37, 1), at] = jnp.sum(dqu, axis=0, keepdims=True)
         total_ref[pl.ds(38, 1), at] = jnp.sum(dqv, axis=0, keepdims=True)
 
+    last = H // 2 - 1
+
     def attention(pbuf):
         load = lambda h: pltpu.make_async_copy(probs.at[h], pbuf.at[h], psem.at[h])
         for h in range(H):
             load(h).start()
+        for cp in second() + later():
+            cp.start()
+        met()
+        for cp in owns:
+            cp.wait()
+        first()
+        for cp in needed:
+            cp.wait()
+        qut[...] = qu[...].T
+        datt_t[...] = datt[...].T
+
         lax.fori_loop(0, H // 2, lambda p, t: (scores(p, pbuf, load), t)[1], 0)
+        for cp in second():
+            cp.wait()
+        qvt[...] = qv[...].T
         lax.fori_loop(0, H // 2, lambda p, t: (queries(p, pbuf), t)[1], 0)
 
-    last = H // 2 - 1
     pl.run_scoped(attention, pltpu.VMEM((H, rows, kv.shape[2] * rows), BF))
+
     def tail(pre_ref, w1, hid_ref, dpre_ref):
-        last_in = [fetch(pre_h, pre_ref), fetch(wn.at[pl.ds(0, 4096), :], w1)]
+        for cp in last_in(pre_ref, w1):
+            cp.start()
         g_low[pl.ds(FLAT["p"], 512), :] = gpost[...].T.astype(BF)
-        for cp in later:
+        for cp in later():
             cp.wait()
         a2t = a2[...].T
         g_low[pl.ds(FLAT["q"], 512), :] = dot(a2t, dq_ref[...]).astype(BF)
@@ -1300,7 +1337,7 @@
         g_low[pl.ds(FLAT["k"], 512), :] = dot_nt(a2t, dkt[...]).astype(BF)
         g_low[pl.ds(FLAT["v"], 512), :] = dot_nt(a2t, dvt[...]).astype(BF)
         advance(groups["q"])
-        for cp in last_in:
+        for cp in last_in(pre_ref, w1):
             cp.wait()
         ffn_hidden(pre_ref, hid_ref)
         after(17)
@@ -1343,13 +1380,14 @@
 
 
 def widen_body(flat, total, bns, *refs):
-    outs, smalls, (ibuf, obuf, isem, osem) = refs[:11], refs[11:21], refs[21:]
+    outs, smalls, (ibuf, obuf, rbuf, isem, osem, rsem) = refs[:11], refs[11:21], refs[21:]
     count = smalls[0].shape[0]
-    smalls[0][...] = total[pl.ds(0, count), :]
-    for i, ref in enumerate(smalls[1:8]):
-        ref[...] = total[pl.ds(count + i, 1), :]
-    for i, ref in enumerate(smalls[8:]):
-        ref[...] = bns[pl.ds(i, 1), :]
+    lines = [pltpu.make_async_copy(total.at[pl.ds(0, count), :], smalls[0], rsem.at[0])]
+    for i, ref in enumerate(smalls[1:]):
+        rbuf[i] = total[pl.ds(count + i, 1), :] if i < 7 else bns[pl.ds(i - 7, 1), :]
+        lines.append(pltpu.make_async_copy(rbuf.at[i], ref, rsem.at[1 + i]))
+    for cp in lines:
+        cp.start()
     step = 512
     n = FLAT_ROWS // step
     loads = [pltpu.make_async_copy(flat.at[pl.ds(i * step, step), :], ibuf.at[i], isem.at[i]) for i in range(n)]
@@ -1372,7 +1410,7 @@
         obuf[i % slots] = ibuf[i].astype(F32)
         stores.append(pltpu.make_async_copy(obuf.at[i % slots], dst, osem.at[i % slots]))
         stores[-1].start()
-    for cp in stores[-slots:]:
+    for cp in stores[-slots:] + lines:
         cp.wait()
 
 
@@ -1465,8 +1503,8 @@
         out_shape=[jax.ShapeDtypeStruct(r.shape, F32) for r in raws]
         + [jax.ShapeDtypeStruct((count, width), F32)] + [jax.ShapeDtypeStruct((1, width), F32)] * 9,
         in_specs=[pl.BlockSpec(memory_space=pl.ANY)] + [pl.BlockSpec(memory_space=pltpu.VMEM)] * 2,
-        out_specs=[pl.BlockSpec(memory_space=pl.ANY)] * 11 + [pl.BlockSpec(memory_space=pltpu.VMEM)] * 10,
-        scratch_shapes=[pltpu.VMEM((24, 512, width), BF), pltpu.VMEM((4, 512, width), F32), DMA((24,)), DMA((4,))],
+        out_specs=[pl.BlockSpec(memory_space=pl.ANY)] * 21,
+        scratch_shapes=[pltpu.VMEM((24, 512, width), BF), pltpu.VMEM((4, 512, width), F32), pltpu.VMEM((9, 1, width), F32), DMA((24,)), DMA((4,)), DMA((10,))],
         compiler_params=pltpu.CompilerParams(vmem_limit_bytes=VMEM_LIMIT),
         name="widen",
     )(flat, total, bns)

time: 295 us -> 284 us (0.963)
  Pallas kernels: 291 us -> 281 us
    pallas_call x3, Pallas kernels: 277 us -> 267 us  [remote(): pl.pallas_call(body, out_shape=[jax.ShapeDtypeStruct(s, d) for s, d, _ in...]
where the time goes in v2:
time: 284 us; the launch traced here: 283 us
  Pallas kernels  281 us (99%)
    pallas_call x3, Pallas kernels, remote(): pl.pallas_call(body, out_shape=[jax.ShapeDtypeStruct(s, d) for s, d, _ in...  267 us
    pallas_call x1, Pallas kernels, local(): pl.pallas_call(widen_body, out_shape=[jax.ShapeDtypeStruct(r.shape, F32)...  13.3 us

profile of v2, /device:TPU:0, one launch (start us, length us, event | category | flops | bytes accessed | tf_op | source)
XLA Modules:
  0.0 283.5 jit_solution(13085451888373415830)
XLA Ops:
  1.3 99.6 %early.1 = (bf16[12288,512]{1,0:T(8,128)(2,1)}, f32[384,512]{1,0:T(8,128)}, f32[384,2048]{1,0:T(8,128)}, bf16[384,512]{1,0:T(8,128)(2,1)}, bf16[384,512]{1,0:T(8...) custom-call(s32[1]{0:T(128)S(6)} %copy.50.refs_0_.lens, ...), custom_call_target="tpu_custom_call" | custom-call | tf_op jit(solution)/shard_map/early/pallas_call | solution.py:1423
  100.9 45.0 %middle.1 = (bf16[384,512]{1,0:T(8,128)(2,1)}, f32[384,512]{1,0:T(8,128)}, bf16[384,512]{1,0:T(8,128)(2,1)}, bf16[6144,512]{1,0:T(8,128)(2,1)}, f32[40,512]{1,0:...) custom-call(s32[1]{0:T(128)S(6)} %copy.50.refs_0_.lens, bf16[384,512]{1,0:T(8,128)(2,1)} %get-tuple-element.66.att.att_h, ...), custom_call_target="tpu_custom_call" | custom-call | tf_op jit(solution)/shard_map/middle/pallas_call | solution.py:1423
  146.0 122.7 %late.1 = (bf16[384,512]{1,0:T(8,128)(2,1)}, bf16[12288,512]{1,0:T(8,128)(2,1)}, f32[40,512]{1,0:T(8,128)}) custom-call(bf16[384,512]{1,0:T(8,128)(2,1)} %get-tuple-element.70.qu_h, bf16[384,512]{1,0:T(8,128)(2,1)} %get-tuple-element.71.qv_h, bf16[4,2,4,384,128]{4,3,2,1,0:T(8,128)(2,1)} %get-tuple-element.72.kv_h, bf16[12288,512]{1,0:T(8,128)(2,1)} %get-tuple-element.68.wn, ...), custom_call_target="tpu_custom_call" | custom-call | tf_op jit(solution)/shard_map/late/pallas_call | solution.py:1423
  268.6 0.0 copy-start
  268.6 0.0 copy-start.1
  268.7 13.3 %widen.1 = (f32[512,2048]{1,0:T(8,128)}, f32[2048,512]{1,0:T(8,128)}, f32[512,512]{1,0:T(8,128)}, f32[512,512]{1,0:T(8,128)}, f32[512,512]{1,0:T(8,128)}, /*inde...) custom-call(bf16[12288,512]{1,0:T(8,128)(2,1)} %get-tuple-element.85, ...), custom_call_target="tpu_custom_call" | custom-call | tf_op jit(solution)/shard_map/widen/pallas_call | solution.py:1501
  281.9 0.0 copy-done
  282.0 0.7 copy.51
  282.7 0.0 copy-done.1
  282.7 0.7 copy.52
Async XLA Ops:
  268.6 13.3 %copy-start = (bf16[384,512]{1,0:T(8,128)(2,1)S(1)}, bf16[384,512]{1,0:T(8,128)(2,1)}, u32[]{:S(2)}) copy-start(bf16[384,512]{1,0:T(8,128)(2,1)} %get-tuple-element.69) | copy-start | bytes 1179652
  268.6 14.1 %copy-start.1 = (bf16[384,512]{1,0:T(8,128)(2,1)S(1)}, bf16[384,512]{1,0:T(8,128)(2,1)}, u32[]{:S(2)}) copy-start(bf16[384,512]{1,0:T(8,128)(2,1)} %get-tuple-element.84) | copy-start | bytes 1179652

commit v3 on v2

--- a/solution.py
+++ b/solution.py
@@ -317,27 +317,29 @@
 NAMES = ("f2i", "f2o", "o", "q", "f1o", "f1i")
 AXES = {"A": ("y", "x", "z"), "B": ("x", "y", "z"), "X": ("z", "x", "y"), "Y": ("z", "y", "x")}
 FRONT = ("f2i",)
-LANES = {"f2i": "A2 B2", "f2o": "B1 A1 B1 A1", "o": "A1 B1 A1 B1", "q": "A1 B1 A1 X1", "f1o": "A2 B1 X1", "f1i": "A1 B2 Y1"}
+LANES = {"f2i": "A2 B1 B1", "f2o": "A2 B1 X1", "o": "A2 B1 X1", "q": "A1 B1 B1 Y1", "f1o": "A1 B1 B1 Y1", "f1i": "A1 B1 A1 B1"}
 TURNS = {
-    -1: (4, 5, 6, 7, 8, 9, 10, 11, 0, 1,),
-    0: (4, 5, 6,),
-    1: (8, 0, 10,),
-    2: (1, 7,),
-    3: (9,),
-    4: (0, 4,),
+    -1: (4, 5, 6, 8, 9, 10, 0, 1, 2,),
+    0: (5, 6, 9,),
+    1: (4, 8, 10,),
+    3: (5, 0,),
+    4: (9,),
     5: (6, 1,),
-    8: (4, 9, 6,),
-    9: (1,),
-    11: (9, 4, 8,),
-    12: (6,),
-    13: (5, 0,),
-    15: (8, 4, 10,),
-    16: (5, 11, 9,),
-    17: (8, 0, 4,),
-    18: (12, 5, 13,),
-    19: (14, 8, 15,),
-    20: (16, 17, 18,),
-    21: (12, 13, 10, 7, 0, 4, 14, 22, 20, 5, 4, 12, 21, 13, 17, 10, 18, 7, 0, 14, 16, 8, 11, 17, 12, 18, 9, 20, 5, 11, 13, 18, 16, 15, 1, 8, 14, 6, 7, 10, 8, 21, 20, 15, 17, 12, 5, 22, 15, 5, 11, 10, 13, 9, 21, 22, 12, 14, 20, 1, 17, 13, 16, 22, 10, 9, 18, 1, 11, 21, 14, 20, 10, 9, 22, 12, 17, 18, 16, 12, 13, 20, 22, 21, 13, 14, 6, 14, 7, 17, 16, 17, 15, 18, 20, 11, 21, 7, 18, 20, 6, 22, 15, 6, 22, 11, 16, 7, 11, 15, 21, 7, 16, 15, 21,),
+    6: (2,),
+    7: (5,),
+    8: (6, 9, 0,),
+    10: (4, 1, 2,),
+    11: (6,),
+    12: (5, 9, 8,),
+    13: (10, 1, 2,),
+    14: (4, 0, 6,),
+    15: (10, 5, 9,),
+    16: (8, 1, 2,),
+    17: (4, 10, 0,),
+    18: (12, 8, 13,),
+    19: (14, 15, 4,),
+    20: (16, 19, 17,),
+    21: (18, 12, 13, 14, 15, 6, 0, 1, 2, 20, 21, 22, 17, 23, 0, 12, 1, 2, 13, 14, 18, 16, 6, 15, 17, 12, 8, 21, 10, 13, 19, 6, 23, 20, 16, 14, 4, 18, 22, 19, 17, 15, 21, 13, 12, 5, 20, 8, 23, 22, 19, 14, 16, 9, 18, 13, 21, 5, 20, 17, 15, 22, 5, 23, 4, 16, 14, 19, 10, 9, 18, 13, 15, 21, 4, 9, 20, 13, 19, 22, 12, 23, 16, 17, 14, 18, 8, 14, 20, 8, 21, 17, 23, 22, 17, 18, 12, 10, 16, 15, 18, 19, 12, 21, 10, 20, 16, 15, 23, 19, 22, 21, 20, 23, 22,),
 }
 
 
@@ -872,20 +874,13 @@
     lax.fori_loop(0, rows // block, one, 0)
 
 
-def bn_stats(sums):
-    total = sums[2:3, :]
-    mu = sums[0:1, :] / total
-    var = sums[1:2, :] / total - mu * mu
-    return mu, lax.rsqrt(var + EPS), total
-
-
 class Totals:
     @staticmethod
-    def scratch(tms, slots, width):
+    def scratch(tms, slots, packed):
         n = tms + slots - 2
         return [
-            pltpu.VMEM((tms, 8, width), F32),
-            pltpu.VMEM((slots, 8, width), F32),
+            pltpu.VMEM((tms, packed, LANE), F32),
+            pltpu.VMEM((slots, packed, LANE), F32),
             pltpu.SemaphoreType.DMA((n,)),
             pltpu.SemaphoreType.DMA((n,)),
         ]
@@ -931,6 +926,15 @@
         for j in range(1, buf.shape[0]):
             value = value + buf[j]
         return value
+
+
+def packed(rows):
+    return jnp.concatenate([row[:, at : at + LANE] for row in rows for at in range(0, row.shape[1], LANE)], axis=0)
+
+
+def unpacked(value, row, width):
+    n = width // LANE
+    return jnp.concatenate([value[row * n + j : row * n + j + 1, :] for j in range(n)], axis=1)
 
 
 def greet_rows(pc, tms, slots):
@@ -989,19 +993,19 @@
     dwo = dwo_ref[...]
     dwv = dwo * ok
     totals[0].begin(
-        jnp.concatenate(
+        packed(
             [
                 jnp.sum(dwv, axis=0, keepdims=True),
                 jnp.sum(dwv * dwv, axis=0, keepdims=True),
-                jnp.zeros((1, width), F32) + jnp.sum(ok, axis=0, keepdims=True),
-                jnp.zeros((5, width), F32),
-            ],
-            axis=0,
+                jnp.zeros((1, 2 * width), F32) + jnp.sum(ok, axis=0, keepdims=True),
+            ]
         )
     )
     totals[0].turn()
     sums = totals[0].done()
-    mu, inv, total = bn_stats(sums)
+    total = sums[2 * width // LANE : 2 * width // LANE + 1, 0:1]
+    mu = unpacked(sums, 0, width) / total
+    inv = lax.rsqrt(unpacked(sums, 1, width) / total - mu * mu + EPS)
     xhat = (dwo_ref[...] - mu) * inv
     sw, slope = swish_and_slope(xhat * bn_gain[...] + bn_bias[...])
     sw = sw.astype(BF)
@@ -1021,11 +1025,7 @@
     dx3 = dx4 + back
     g3 = dx3.astype(BF)
     dbn = dot_nt(g3, w_co[...]) * slope
-    totals[1].begin(
-        jnp.concatenate(
-            [jnp.sum(dbn * xhat, axis=0, keepdims=True), jnp.sum(dbn, axis=0, keepdims=True), jnp.zeros((6, width), F32)], axis=0
-        )
-    )
+    totals[1].begin(packed([jnp.sum(dbn * xhat, axis=0, keepdims=True), jnp.sum(dbn, axis=0, keepdims=True)]))
     part = lambda name: g_ref.at[pl.ds(MID[name], GROUP), :]
     ffn_in_grad(a4, dpre_ref, part("f2i"))
     totals[1].turn()
@@ -1036,8 +1036,11 @@
         if name not in FRONT:
             outs.append(put(part(name), g_h.at[pl.ds(MID[name], GROUP), :]))
     sums2 = totals[1].done()
-    bns_ref[...] = sums2
-    ddwo_ref[...] = (bn_gain[...] * inv * (dbn - ok * (sums2[1:2, :] + xhat * sums2[0:1, :]) / total)).astype(BF)
+    gain_sum, bias_sum = unpacked(sums2, 0, width), unpacked(sums2, 1, width)
+    bns_ref[0:1, :] = gain_sum
+    bns_ref[1:2, :] = bias_sum
+    bns_ref[2:8, :] = jnp.zeros((6, width), F32)
+    ddwo_ref[...] = (bn_gain[...] * inv * (dbn - ok * (bias_sum + xhat * gain_sum) / total)).astype(BF)
     cp = halo(ddwo_ref.at[pl.ds(0, count), :], late, 1, -1)
     cp.start()
     advance(flows)
@@ -1479,7 +1482,7 @@
            pltpu.VMEM((count, 8, LANE), F32), pltpu.VMEM((rows, width), F32), V((max(1, len(FRONT)), GROUP // 2, width)),
            V((rows, width)), V((rows, width), F32), V((rows, width)), V((3 * GROUP, width)),
            V((rows, hidden)), V((rows, hidden)), DMA((7,))]
-        + Totals.scratch(tms, slots, width) * 2 + flat_list([flat_list(flow_scratch(size, n, "front")) for n in FRONT]),
+        + Totals.scratch(tms, slots, 4 * width // LANE) + Totals.scratch(tms, slots, 2 * width // LANE) + flat_list([flat_list(flow_scratch(size, n, "front")) for n in FRONT]),
         "middle",
     )
     dx0, flat, total = remote(

time: 284 us -> 281 us (0.989)
  Pallas kernels: 281 us -> 278 us
where the time goes in v3:
time: 281 us
  Pallas kernels  278 us (99%)
    pallas_call x3, Pallas kernels, remote(): pl.pallas_call(body, out_shape=[jax.ShapeDtypeStruct(s, d) for s, d, _ in...  265 us
    pallas_call x1, Pallas kernels, local(): pl.pallas_call(widen_body, out_shape=[jax.ShapeDtypeStruct(r.shape, F32)...  13.3 us

profile of v3, /device:TPU:0, one launch (start us, length us, event | category | flops | bytes accessed | tf_op | source)
XLA Modules:
  0.0 281.1 jit_solution(16510954986500306135)
XLA Ops:
  1.3 99.6 %early.1 = (bf16[12288,512]{1,0:T(8,128)(2,1)}, f32[384,512]{1,0:T(8,128)}, f32[384,2048]{1,0:T(8,128)}, bf16[384,512]{1,0:T(8,128)(2,1)}, bf16[384,512]{1,0:T(8...) custom-call(s32[1]{0:T(128)S(6)} %copy.50.refs_0_.lens, ...), custom_call_target="tpu_custom_call" | custom-call | tf_op jit(solution)/shard_map/early/pallas_call | solution.py:1426
  100.9 43.7 %middle.1 = (bf16[384,512]{1,0:T(8,128)(2,1)}, f32[384,512]{1,0:T(8,128)}, bf16[384,512]{1,0:T(8,128)(2,1)}, bf16[6144,512]{1,0:T(8,128)(2,1)}, f32[40,512]{1,0:...) custom-call(s32[1]{0:T(128)S(6)} %copy.50.refs_0_.lens, bf16[384,512]{1,0:T(8,128)(2,1)} %get-tuple-element.66.att.att_h, ...), custom_call_target="tpu_custom_call" | custom-call | tf_op jit(solution)/shard_map/middle/pallas_call | solution.py:1426
  144.7 121.6 %late.1 = (bf16[384,512]{1,0:T(8,128)(2,1)}, bf16[12288,512]{1,0:T(8,128)(2,1)}, f32[40,512]{1,0:T(8,128)}) custom-call(bf16[384,512]{1,0:T(8,128)(2,1)} %get-tuple-element.70.qu_h, bf16[384,512]{1,0:T(8,128)(2,1)} %get-tuple-element.71.qv_h, bf16[4,2,4,384,128]{4,3,2,1,0:T(8,128)(2,1)} %get-tuple-element.72.kv_h, bf16[12288,512]{1,0:T(8,128)(2,1)} %get-tuple-element.68.wn, ...), custom_call_target="tpu_custom_call" | custom-call | tf_op jit(solution)/shard_map/late/pallas_call | solution.py:1426
  266.3 0.0 copy-start
  266.3 0.0 copy-start.1
  266.3 13.3 %widen.1 = (f32[512,2048]{1,0:T(8,128)}, f32[2048,512]{1,0:T(8,128)}, f32[512,512]{1,0:T(8,128)}, f32[512,512]{1,0:T(8,128)}, f32[512,512]{1,0:T(8,128)}, /*inde...) custom-call(bf16[12288,512]{1,0:T(8,128)(2,1)} %get-tuple-element.85, ...), custom_call_target="tpu_custom_call" | custom-call | tf_op jit(solution)/shard_map/widen/pallas_call | solution.py:1504
  279.6 0.0 copy-done
  279.6 0.7 copy.51
  280.4 0.0 copy-done.1
  280.4 0.7 copy.52
Async XLA Ops:
  266.3 13.3 %copy-start = (bf16[384,512]{1,0:T(8,128)(2,1)S(1)}, bf16[384,512]{1,0:T(8,128)(2,1)}, u32[]{:S(2)}) copy-start(bf16[384,512]{1,0:T(8,128)(2,1)} %get-tuple-element.69) | copy-start | bytes 1179652
  266.3 14.1 %copy-start.1 = (bf16[384,512]{1,0:T(8,128)(2,1)S(1)}, bf16[384,512]{1,0:T(8,128)(2,1)}, u32[]{:S(2)}) copy-start(bf16[384,512]{1,0:T(8,128)(2,1)} %get-tuple-element.84) | copy-start | bytes 1179652

commit v4 on v3

--- a/solution.py
+++ b/solution.py
@@ -317,29 +317,30 @@
 NAMES = ("f2i", "f2o", "o", "q", "f1o", "f1i")
 AXES = {"A": ("y", "x", "z"), "B": ("x", "y", "z"), "X": ("z", "x", "y"), "Y": ("z", "y", "x")}
 FRONT = ("f2i",)
-LANES = {"f2i": "A2 B1 B1", "f2o": "A2 B1 X1", "o": "A2 B1 X1", "q": "A1 B1 B1 Y1", "f1o": "A1 B1 B1 Y1", "f1i": "A1 B1 A1 B1"}
+LANES = {"f2i": "A2 B1 B1", "f2o": "A2 B1 X1", "o": "A2 B1 B1", "q": "A1 B1 B1 Y1", "f1o": "A1 B1 A1 X1", "f1i": "A1 B1 A1 B1"}
 TURNS = {
     -1: (4, 5, 6, 8, 9, 10, 0, 1, 2,),
     0: (5, 6, 9,),
     1: (4, 8, 10,),
-    3: (5, 0,),
-    4: (9,),
+    2: (0, 1,),
+    4: (5, 9, 2,),
     5: (6, 1,),
-    6: (2,),
-    7: (5,),
-    8: (6, 9, 0,),
-    10: (4, 1, 2,),
-    11: (6,),
-    12: (5, 9, 8,),
-    13: (10, 1, 2,),
-    14: (4, 0, 6,),
-    15: (10, 5, 9,),
-    16: (8, 1, 2,),
-    17: (4, 10, 0,),
-    18: (12, 8, 13,),
-    19: (14, 15, 4,),
-    20: (16, 19, 17,),
-    21: (18, 12, 13, 14, 15, 6, 0, 1, 2, 20, 21, 22, 17, 23, 0, 12, 1, 2, 13, 14, 18, 16, 6, 15, 17, 12, 8, 21, 10, 13, 19, 6, 23, 20, 16, 14, 4, 18, 22, 19, 17, 15, 21, 13, 12, 5, 20, 8, 23, 22, 19, 14, 16, 9, 18, 13, 21, 5, 20, 17, 15, 22, 5, 23, 4, 16, 14, 19, 10, 9, 18, 13, 15, 21, 4, 9, 20, 13, 19, 22, 12, 23, 16, 17, 14, 18, 8, 14, 20, 8, 21, 17, 23, 22, 17, 18, 12, 10, 16, 15, 18, 19, 12, 21, 10, 20, 16, 15, 23, 19, 22, 21, 20, 23, 22,),
+    6: (10, 0,),
+    7: (2,),
+    8: (6, 1, 5,),
+    9: (4, 9,),
+    10: (10, 6, 2,),
+    11: (5,),
+    12: (8, 9,),
+    13: (10,),
+    14: (0, 5, 6,),
+    15: (4, 9, 1,),
+    16: (10, 2,),
+    17: (8, 5, 4,),
+    18: (12, 13, 0,),
+    19: (14, 15, 6,),
+    20: (16, 17, 18,),
+    21: (19, 12, 13, 8, 4, 0, 1, 2, 20, 21, 5, 22, 14, 1, 2, 12, 0, 5, 6, 23, 13, 16, 6, 17, 15, 18, 14, 12, 21, 8, 4, 13, 20, 16, 23, 17, 18, 19, 14, 22, 21, 15, 12, 20, 13, 9, 8, 23, 16, 15, 22, 17, 10, 19, 18, 12, 14, 4, 21, 13, 20, 9, 4, 19, 23, 16, 9, 10, 15, 22, 14, 18, 13, 10, 17, 21, 13, 23, 20, 15, 12, 16, 19, 8, 12, 18, 22, 17, 14, 8, 21, 20, 19, 14, 15, 22, 23, 15, 16, 17, 18, 21, 16, 19, 17, 20, 18, 23, 21, 19, 22, 20, 23, 22,),
 }
 
 

time: 281 us -> 279 us (level)
  no operation moved by 1% of the time
where the time goes in v4:
time: 279 us
  Pallas kernels  276 us (99%)
    pallas_call x3, Pallas kernels, remote(): pl.pallas_call(body, out_shape=[jax.ShapeDtypeStruct(s, d) for s, d, _ in...  263 us
    pallas_call x1, Pallas kernels, local(): pl.pallas_call(widen_body, out_shape=[jax.ShapeDtypeStruct(r.shape, F32)...  13.3 us

profile of v4, /device:TPU:0, one launch (start us, length us, event | category | flops | bytes accessed | tf_op | source)
XLA Modules:
  0.0 279.0 jit_solution(15284624691199134717)
XLA Ops:
  1.3 99.6 %early.1 = (bf16[12288,512]{1,0:T(8,128)(2,1)}, f32[384,512]{1,0:T(8,128)}, f32[384,2048]{1,0:T(8,128)}, bf16[384,512]{1,0:T(8,128)(2,1)}, bf16[384,512]{1,0:T(8...) custom-call(s32[1]{0:T(128)S(6)} %copy.50.refs_0_.lens, ...), custom_call_target="tpu_custom_call" | custom-call | tf_op jit(solution)/shard_map/early/pallas_call | solution.py:1427
  100.9 43.7 %middle.1 = (bf16[384,512]{1,0:T(8,128)(2,1)}, f32[384,512]{1,0:T(8,128)}, bf16[384,512]{1,0:T(8,128)(2,1)}, bf16[6144,512]{1,0:T(8,128)(2,1)}, f32[40,512]{1,0:...) custom-call(s32[1]{0:T(128)S(6)} %copy.50.refs_0_.lens, bf16[384,512]{1,0:T(8,128)(2,1)} %get-tuple-element.66.att.att_h, ...), custom_call_target="tpu_custom_call" | custom-call | tf_op jit(solution)/shard_map/middle/pallas_call | solution.py:1427
  144.7 119.5 %late.1 = (bf16[384,512]{1,0:T(8,128)(2,1)}, bf16[12288,512]{1,0:T(8,128)(2,1)}, f32[40,512]{1,0:T(8,128)}) custom-call(bf16[384,512]{1,0:T(8,128)(2,1)} %get-tuple-element.70.qu_h, bf16[384,512]{1,0:T(8,128)(2,1)} %get-tuple-element.71.qv_h, bf16[4,2,4,384,128]{4,3,2,1,0:T(8,128)(2,1)} %get-tuple-element.72.kv_h, bf16[12288,512]{1,0:T(8,128)(2,1)} %get-tuple-element.68.wn, ...), custom_call_target="tpu_custom_call" | custom-call | tf_op jit(solution)/shard_map/late/pallas_call | solution.py:1427
  264.2 0.0 copy-start
  264.2 0.0 copy-start.1
  264.2 13.3 %widen.1 = (f32[512,2048]{1,0:T(8,128)}, f32[2048,512]{1,0:T(8,128)}, f32[512,512]{1,0:T(8,128)}, f32[512,512]{1,0:T(8,128)}, f32[512,512]{1,0:T(8,128)}, /*inde...) custom-call(bf16[12288,512]{1,0:T(8,128)(2,1)} %get-tuple-element.85, ...), custom_call_target="tpu_custom_call" | custom-call | tf_op jit(solution)/shard_map/widen/pallas_call | solution.py:1505
  277.5 0.0 copy-done
  277.5 0.7 copy.51
  278.2 0.0 copy-done.1
  278.2 0.7 copy.52
Async XLA Ops:
  264.2 13.3 %copy-start = (bf16[384,512]{1,0:T(8,128)(2,1)S(1)}, bf16[384,512]{1,0:T(8,128)(2,1)}, u32[]{:S(2)}) copy-start(bf16[384,512]{1,0:T(8,128)(2,1)} %get-tuple-element.69) | copy-start | bytes 1179652
  264.2 14.1 %copy-start.1 = (bf16[384,512]{1,0:T(8,128)(2,1)S(1)}, bf16[384,512]{1,0:T(8,128)(2,1)}, u32[]{:S(2)}) copy-start(bf16[384,512]{1,0:T(8,128)(2,1)} %get-tuple-element.84) | copy-start | bytes 1179652

commit v5 on v4

--- a/solution.py
+++ b/solution.py
@@ -1508,7 +1508,7 @@
         + [jax.ShapeDtypeStruct((count, width), F32)] + [jax.ShapeDtypeStruct((1, width), F32)] * 9,
         in_specs=[pl.BlockSpec(memory_space=pl.ANY)] + [pl.BlockSpec(memory_space=pltpu.VMEM)] * 2,
         out_specs=[pl.BlockSpec(memory_space=pl.ANY)] * 21,
-        scratch_shapes=[pltpu.VMEM((24, 512, width), BF), pltpu.VMEM((4, 512, width), F32), pltpu.VMEM((9, 1, width), F32), DMA((24,)), DMA((4,)), DMA((10,))],
+        scratch_shapes=[pltpu.VMEM((24, 512, width), BF), pltpu.VMEM((12, 512, width), F32), pltpu.VMEM((9, 1, width), F32), DMA((24,)), DMA((12,)), DMA((10,))],
         compiler_params=pltpu.CompilerParams(vmem_limit_bytes=VMEM_LIMIT),
         name="widen",
     )(flat, total, bns)

time: 279 us -> 279 us (level)
  no operation moved by 1% of the time
where the time goes in v5:
time: 279 us
  Pallas kernels  276 us (99%)
    pallas_call x3, Pallas kernels, remote(): pl.pallas_call(body, out_shape=[jax.ShapeDtypeStruct(s, d) for s, d, _ in...  263 us
    pallas_call x1, Pallas kernels, local(): pl.pallas_call(widen_body, out_shape=[jax.ShapeDtypeStruct(r.shape, F32)...  13.4 us

profile of v5, /device:TPU:0, one launch (start us, length us, event | category | flops | bytes accessed | tf_op | source)
XLA Modules:
  0.0 279.1 jit_solution(12474029923777743917)
XLA Ops:
  1.3 99.6 %early.1 = (bf16[12288,512]{1,0:T(8,128)(2,1)}, f32[384,512]{1,0:T(8,128)}, f32[384,2048]{1,0:T(8,128)}, bf16[384,512]{1,0:T(8,128)(2,1)}, bf16[384,512]{1,0:T(8...) custom-call(s32[1]{0:T(128)S(6)} %copy.50.refs_0_.lens, ...), custom_call_target="tpu_custom_call" | custom-call | tf_op jit(solution)/shard_map/early/pallas_call | solution.py:1427
  100.9 43.7 %middle.1 = (bf16[384,512]{1,0:T(8,128)(2,1)}, f32[384,512]{1,0:T(8,128)}, bf16[384,512]{1,0:T(8,128)(2,1)}, bf16[6144,512]{1,0:T(8,128)(2,1)}, f32[40,512]{1,0:...) custom-call(s32[1]{0:T(128)S(6)} %copy.50.refs_0_.lens, bf16[384,512]{1,0:T(8,128)(2,1)} %get-tuple-element.66.att.att_h, ...), custom_call_target="tpu_custom_call" | custom-call | tf_op jit(solution)/shard_map/middle/pallas_call | solution.py:1427
  144.7 119.5 %late.1 = (bf16[384,512]{1,0:T(8,128)(2,1)}, bf16[12288,512]{1,0:T(8,128)(2,1)}, f32[40,512]{1,0:T(8,128)}) custom-call(bf16[384,512]{1,0:T(8,128)(2,1)} %get-tuple-element.70.qu_h, bf16[384,512]{1,0:T(8,128)(2,1)} %get-tuple-element.71.qv_h, bf16[4,2,4,384,128]{4,3,2,1,0:T(8,128)(2,1)} %get-tuple-element.72.kv_h, bf16[12288,512]{1,0:T(8,128)(2,1)} %get-tuple-element.68.wn, ...), custom_call_target="tpu_custom_call" | custom-call | tf_op jit(solution)/shard_map/late/pallas_call | solution.py:1427
  264.2 0.0 copy-start
  264.2 0.0 copy-start.1
  264.2 13.4 %widen.1 = (f32[512,2048]{1,0:T(8,128)}, f32[2048,512]{1,0:T(8,128)}, f32[512,512]{1,0:T(8,128)}, f32[512,512]{1,0:T(8,128)}, f32[512,512]{1,0:T(8,128)}, /*inde...) custom-call(bf16[12288,512]{1,0:T(8,128)(2,1)} %get-tuple-element.85, ...), custom_call_target="tpu_custom_call" | custom-call | tf_op jit(solution)/shard_map/widen/pallas_call | solution.py:1505
  277.6 0.0 copy-done
  277.6 0.7 copy.51
  278.3 0.0 copy-done.1
  278.3 0.7 copy.52
Async XLA Ops:
  264.2 13.4 %copy-start = (bf16[384,512]{1,0:T(8,128)(2,1)S(1)}, bf16[384,512]{1,0:T(8,128)(2,1)}, u32[]{:S(2)}) copy-start(bf16[384,512]{1,0:T(8,128)(2,1)} %get-tuple-element.69) | copy-start | bytes 1179652
  264.2 14.1 %copy-start.1 = (bf16[384,512]{1,0:T(8,128)(2,1)S(1)}, bf16[384,512]{1,0:T(8,128)(2,1)}, u32[]{:S(2)}) copy-start(bf16[384,512]{1,0:T(8,128)(2,1)} %get-tuple-element.84) | copy-start | bytes 1179652
